TPU v7x, 256 devices: a whole 4x4x8 slice. The times are simulated.
256 devices in a mesh: row: 8 (over x, y_hi), col: 32 (over y_lo, z, core).
Axes of the slice: x: 4, y: 4 (y_hi: 2, y_lo: 2; y = y_hi * 2 + y_lo), z: 8, core: 2. Of those that a mesh axis runs over, the one named last changes fastest.
Arguments:
- features: bfloat16 [65536, 256], P(('row', 'col')), may hold values from -6 to 6
- weight: bfloat16 [256, 256], replicated, may hold values from -0.375 to 0.375
- cotangent: bfloat16 [65536, 256], P(('row', 'col')), may hold values from -6 to 6
- block_values: bfloat16 [8, 32, 32, 8, 128, 128], P('row', 'col'), may hold values from -0.046875 to 0.046875
- source_block: int32 [8, 32, 32, 8], P('row', 'col'), may hold values from 0 to 1
- target_block: int32 [8, 32, 32, 8], P('row', 'col'), may hold values from 0 to 15
- block_counts: int32 [8, 32, 32], P('row', 'col'), may hold values from 1 to 8, as said below
- block_order: int32 [256, 2], P(('row', 'col')), may hold values from 0 to 1, each once within a row
Outputs:
- activated: bfloat16 [65536, 256], P(('row', 'col'))
- input_grad: bfloat16 [65536, 256], P(('row', 'col'))
- weight_grad: bfloat16 [256, 256], replicated
Inputs may be any that keep to these rules, and one draw needn't show every extreme that they name: `block_counts`: in every tile at least one source group has all 8 slots live; the others have from 1 up.
All inputs are finite; a program needn't handle non-finite values.
Results may differ from a plain program's by a relative error of at most 0.0067.
Values may be sent and summed in bfloat16 or wider, within the bound.
No kernel may reach another device: no remote copies, remote signals or barrier semaphores. Data moves between devices by JAX's collectives and lax.ppermute only.
A program may use at most 128 MiB of HBM per device.

v0:
```python
import jax
import jax.numpy as jnp
from jax import lax
from jax.sharding import PartitionSpec as P

HIGH = lax.Precision.HIGHEST


def group_width():
    return 4


def forward_block(totals, vals, src, dst, live, stripe_blocks):
    local_blocks = stripe_blocks.shape[1]
    dest_blocks = totals.shape[0]
    src_hot = (src[..., None] == jnp.arange(local_blocks, dtype=jnp.int32)).astype(jnp.bfloat16)
    picked = jnp.einsum(
        "gkq,gqjf->gkjf", src_hot, stripe_blocks, preferred_element_type=jnp.float32
    ).astype(jnp.bfloat16)
    products = jnp.einsum("gkij,gkjf->gkif", vals, picked, preferred_element_type=jnp.float32)
    slot_ids = jnp.arange(vals.shape[1], dtype=jnp.int32)
    live_hot = slot_ids[None, :] < live[:, None]
    dst_hot = (
        (dst[..., None] == jnp.arange(dest_blocks, dtype=jnp.int32)) & live_hot[..., None]
    ).astype(jnp.float32)
    return totals + jnp.einsum("gkt,gkif->tif", dst_hot, products, precision=HIGH)


def body(
    features, weight, cotangent, block_values, source_block, target_block, block_counts, block_order
):
    col_count = lax.axis_size("col")
    row_count = lax.axis_size("row")
    local_blocks = block_order.shape[1]
    block_size = block_values.shape[-1]
    feat_width = features.shape[1]
    slot_total = block_values.shape[3]
    local_rows = features.shape[0]
    dest_blocks = row_count * local_blocks
    tile_values = block_values[0, 0]
    src_table = source_block[0, 0]
    dst_table = target_block[0, 0]
    live_counts = block_counts[0, 0]
    local_order = block_order[0]
    slot_ids = jnp.arange(slot_total, dtype=jnp.int32)
    order_hot = (local_order[:, None] == jnp.arange(local_blocks, dtype=jnp.int32)[None, :]).astype(
        jnp.bfloat16
    )
    feat_blocks = features.reshape(local_blocks, block_size, feat_width)
    ordered = jnp.einsum(
        "qb,bif->qif", order_hot, feat_blocks, preferred_element_type=jnp.float32
    ).astype(jnp.bfloat16)
    ordered = ordered.reshape(local_rows, feat_width)
    zeros_acc = jnp.zeros((dest_blocks, block_size, feat_width), jnp.float32)
    stripe = lax.all_gather(ordered, "col", axis=0, tiled=True)
    stripe = stripe.reshape(col_count, local_blocks, block_size, feat_width)
    stripe_blocks = stripe
    width = group_width()

    def many_groups(i, inner):
        begin = i * width
        group = 0 + begin
        return forward_block(
            inner,
            lax.dynamic_slice_in_dim(tile_values, group, width, 0),
            lax.dynamic_slice_in_dim(src_table, group, width, 0),
            lax.dynamic_slice_in_dim(dst_table, group, width, 0),
            lax.dynamic_slice_in_dim(live_counts, group, width, 0),
            lax.dynamic_slice_in_dim(stripe_blocks, begin, width, 0),
        )

    totals = lax.fori_loop(0, col_count // width, many_groups, zeros_acc)
    summed = lax.psum_scatter(
        totals.reshape(dest_blocks * block_size, feat_width), "row", scatter_dimension=0, tiled=True
    )
    aggregate = summed.astype(jnp.bfloat16)
    preact = jnp.dot(aggregate, weight, preferred_element_type=jnp.float32)
    activated = jax.nn.silu(preact).astype(jnp.bfloat16)
    gate_sig = jax.nn.sigmoid(preact)
    delta = (cotangent.astype(jnp.float32) * gate_sig * (1.0 + preact * (1.0 - gate_sig))).astype(
        jnp.bfloat16
    )
    local_weight = lax.dot_general(
        aggregate, delta, (((0,), (0,)), ((), ())), preferred_element_type=jnp.float32
    )
    total_nodes = local_rows * col_count * row_count
    weight_total = lax.psum(local_weight, ("row", "col")) / jnp.sqrt(jnp.float32(total_nodes))
    weight_grad = weight_total.astype(jnp.bfloat16)
    back = lax.dot_general(
        delta, weight, (((1,), (1,)), ((), ())), preferred_element_type=jnp.float32
    )
    back = back.astype(jnp.bfloat16)
    gathered = lax.all_gather(back, "row", axis=0, tiled=True).reshape(
        dest_blocks, block_size, feat_width
    )
    dest_ids = jnp.arange(dest_blocks, dtype=jnp.int32)
    local_ids = jnp.arange(local_blocks, dtype=jnp.int32)

    def backward_group(group):
        tile_vals = tile_values[group]
        src_idx = src_table[group]
        dst_idx = dst_table[group]
        live_count = live_counts[group]
        pick_hot = (dst_idx[:, None] == dest_ids[None, :]).astype(jnp.bfloat16)
        picked = jnp.einsum(
            "kt,tjf->kjf", pick_hot, gathered, preferred_element_type=jnp.float32
        ).astype(jnp.bfloat16)
        products = jnp.einsum("kji,kjf->kif", tile_vals, picked, preferred_element_type=jnp.float32)
        live_hot = slot_ids < live_count
        src_hot = ((src_idx[:, None] == local_ids[None, :]) & live_hot[:, None]).astype(jnp.float32)
        return jnp.einsum("kq,kif->qif", src_hot, products, precision=HIGH)

    group_list = jnp.arange(lax.axis_size("col") * local_rows // local_rows, dtype=jnp.int32)
    owned_rows = lax.psum_scatter(
        lax.map(backward_group, group_list).reshape(lax.axis_size("col") * local_rows, feat_width),
        "col",
        scatter_dimension=0,
        tiled=True,
    )
    owned_rows = owned_rows.reshape(local_blocks, block_size, feat_width)
    natural = jnp.einsum("qb,qif->bif", order_hot.astype(jnp.float32), owned_rows, precision=HIGH)
    input_grad = natural.reshape(local_rows, feat_width).astype(jnp.bfloat16)
    return (activated, input_grad, weight_grad)


def solution(mesh):
    in_specs = (
        P(("row", "col"), None),
        P(),
        P(("row", "col"), None),
        P("row", "col", None, None, None, None),
        P("row", "col", None, None),
        P("row", "col", None, None),
        P("row", "col", None),
        P(("row", "col"), None),
    )
    out_specs = (P(("row", "col"), None), P(("row", "col"), None), P())
    return jax.shard_map(body, mesh=mesh, in_specs=in_specs, out_specs=out_specs, check_vma=False)
```

profile of v0, /device:TPU:4, one launch (start us, length us, event | category | flops | bytes accessed | tf_op | source)
XLA Modules:
  0.0 745.3 jit_solution(665155966966914618)
XLA Ops:
  10.0 70.2 %all-gather.3.cloned.1.call-done = bf16[8192,256]{1,0:T(8,128)(2,1)} async-done(((bf16[256,256]{1,0:T(8,128)(2,1)}), bf16[8192,256]{1,0:T(8,128)(2,1)}) %all-gather.3.cloned.1.call-update) | async-done | bytes 4194320 | tf_op jit(solution)/shard_map/all_gather | solution.py:55
  80.2 104.9 %while.26 = (s32[]{:T(128)}, f32[16,128,256]{2,0,1:T(8,128)S(1)}, s32[32,8]{1,0:T(8,128)S(1)}, s32[32]{0:T(128)}, bf16[32,8,128,128]{3,2,1,0:T(8,128)(2,1)}, /*i...) while((s32[]{:T(128)}, f32[16,128,256]{2,0,1:T(8,128)S(1)}, ...), condition=%wide.region_1.0_spmd.clone, body=%wide.region_0.0_spmd.clone.sunk | while | flops 475006048 | bytes 19400516 | solution.py:72
  82.9 3.9 fusion.82
  87.0 6.3 bitcast_add_fusion.2
  96.1 3.9 fusion.82
  100.2 6.3 bitcast_add_fusion.2
  109.2 3.9 fusion.82
  113.3 6.3 bitcast_add_fusion.2
  122.3 3.9 fusion.82
  126.4 6.3 bitcast_add_fusion.2
  135.4 3.9 fusion.82
  139.5 6.3 bitcast_add_fusion.2
  148.5 3.9 fusion.82
  152.6 6.3 bitcast_add_fusion.2
  161.7 3.9 fusion.82
  165.8 6.3 bitcast_add_fusion.2
  174.8 3.9 fusion.82
  178.9 6.3 bitcast_add_fusion.2
  185.2 2.5 copy.21
  187.8 78.7 %reduce-scatter.3.cloned.1.call-done = f32[256,256]{1,0:T(8,128)} async-done(((f32[2048,256]{1,0:T(8,128)}), f32[256,256]{1,0:T(8,128)}) %reduce-scatter.3.cloned.1.call-update) | async-done | bytes 262160 | tf_op jit(solution)/shard_map/reduce_scatter | solution.py:73
  271.5 50.0 %all-gather.5.cloned.1.call-done = bf16[2048,256]{1,0:T(8,128)(2,1)} async-done(((bf16[256,256]{1,0:T(8,128)(2,1)}), bf16[2048,256]{1,0:T(8,128)(2,1)}) %all-gather.5.cloned.1.call-update) | async-done | bytes 1048592 | tf_op jit(solution)/shard_map/all_gather | solution.py:93
  321.4 285.2 %while.25 = (s32[]{:T(128)}, f32[32,2,128,256]{3,2,1,0:T(8,128)}, s32[32]{0:T(128)S(1)}, s32[32,8]{1,0:T(8,128)S(1)}, s32[32]{0:T(128)S(1)}, /*index=5*/bf16[32,...) while((s32[]{:T(128)}, f32[32,2,128,256]{3,2,1,0:T(8,128)}, ...), condition=%wide.region_4.5_spmd.clone, body=%wide.region_3.4_spmd.clone.sunk | while | flops 81789096 | bytes 5243779 | solution.py:115
  359.6 1.9 fusion.74
  608.2 128.2 %reduce-scatter.5.cloned.1.call-done = f32[256,256]{1,0:T(8,128)} async-done(((f32[8192,256]{1,0:T(8,128)}), f32[256,256]{1,0:T(8,128)}) %reduce-scatter.5.cloned.1.call-update) | async-done | bytes 262160 | tf_op jit(solution)/shard_map/reduce_scatter | solution.py:114
  (361 shorter events, 254.7 us)
Async XLA Ops:
  7.2 259.4 %copy-start = (bf16[256,256]{1,0:T(8,128)(2,1)S(1)}, bf16[256,256]{1,0:T(8,128)(2,1)}, u32[]{:S(2)}) copy-start(bf16[256,256]{1,0:T(8,128)(2,1)} %param.13) | copy-start | bytes 393220
  7.2 73.1 %all-gather.3.cloned.1.call-start = ((), (), s32[]{:S(2)}) async-start(), calls=%async_computation.2 | async-start | bytes 4325376 | tf_op jit(solution)/shard_map/all_gather | solution.py:55
  9.2 257.3 %reduce-scatter.3.cloned.1.call-start = ((), (), s32[]{:S(2)}) async-start(), calls=%async_computation.3 | async-start | bytes 2359296 | tf_op jit(solution)/shard_map/reduce_scatter | solution.py:73
  82.9 3.9 copy-start.3
  96.1 3.9 copy-start.3
  109.2 3.9 copy-start.3
  122.3 3.9 copy-start.3
  135.4 3.9 copy-start.3
  148.5 3.9 copy-start.3
  161.7 3.9 copy-start.3
  174.8 3.9 copy-start.3
  185.2 81.4 %copy-start.2 = (bf16[256,256]{1,0:T(8,128)(2,1)S(1)}, bf16[256,256]{1,0:T(8,128)(2,1)}, u32[]{:S(2)}) copy-start(bf16[256,256]{1,0:T(8,128)(2,1)} %param.14) | copy-start | bytes 393220
  185.2 84.2 %copy-start.1 = (s32[32,8]{0,1:T(8,128)S(1)}, s32[32,8]{0,1:T(8,128)}, u32[]{:S(2)}) copy-start(s32[32,8]{0,1:T(8,128)} %get-tuple-element.462) | copy-start | bytes 3076
  185.2 136.2 %copy-start.4 = (s32[32]{0:T(128)S(1)}, s32[32]{0:T(128)}, u32[]{:S(2)}) copy-start(s32[32]{0:T(128)} %get-tuple-element.465) | copy-start | bytes 388
  187.8 133.6 %all-gather.5.cloned.1.call-start = ((), (), s32[]{:S(2)}) async-start(), calls=%async_computation.4 | async-start | bytes 1179648 | tf_op jit(solution)/shard_map/all_gather | solution.py:93
  269.4 337.3 %all-reduce.2.cloned.1.call-start = ((), (), s32[]{:S(2)}) async-start(), calls=%async_computation.6 | async-start | bytes 524288 | tf_op jit(solution)/shard_map/psum | solution.py:87
  271.4 465.0 %reduce-scatter.5.cloned.1.call-start = ((), (), s32[]{:S(2)}) async-start(), calls=%async_computation.5 | async-start | bytes 8650752 | tf_op jit(solution)/shard_map/reduce_scatter | solution.py:114
  606.6 129.9 %copy-start.5 = (s32[1,2]{1,0:T(1,128)S(1)}, s32[1,2]{1,0:T(1,128)}, u32[]{:S(2)}) copy-start(s32[1,2]{1,0:T(1,128)} %param.19) | copy-start | bytes 28
Sparse Core Ops, SparseCore 0:
  10.4 69.7 all-gather.2
  187.9 78.5 reduce-scatter.2
  270.1 51.2 all-gather.4
  327.6 250.9 all-reduce.1
  606.7 129.6 reduce-scatter.4
where the time goes:
time: 750 us; the launch traced here: 745 us
  waiting for transfers between devices  327 us (44%)
  matrix products  235 us (31%)
  local copies, waits for them, and re-layouts  82.3 us (11%)
  loops' own time  63.5 us (8%)
  other arithmetic  23 us (3%)
  between operations  13.9 us (2%)
    reduce_scatter x1, waiting for transfers between devices, body(): lax.psum_scatter(lax.map(backward_group, group_list).reshape(lax.axis_siz...  128 us
    reduce_scatter x1, waiting for transfers between devices, body(): lax.psum_scatter(totals.reshape(dest_blocks * block_size, feat_width), 'r...  78.7 us
    all_gather x1, waiting for transfers between devices, body(): stripe = lax.all_gather(ordered, 'col', axis=0, tiled=True)  70.2 us
    another operation x1, loops' own time, body(): lax.map(backward_group, group_list)  63.1 us
    dot_general x32, matrix products, backward_group(): jnp.einsum('kt,tjf->kjf', pick_hot, gathered, preferred_element_type=jnp....  60.6 us
    dot_general x8, matrix products, forward_block(): jnp.einsum('gkt,gkif->tif', dst_hot, products, precision=HIGH)  50.4 us
    all_gather x1, waiting for transfers between devices, body(): lax.all_gather(back, 'row', axis=0, tiled=True)  50 us
    dot_general x32, matrix products, backward_group(): jnp.einsum('kji,kjf->kif', tile_vals, picked, preferred_element_type=jnp....  41.9 us
  transfers between devices with their start and end apart: 5, of which 4 were waited for; matrix products, arithmetic and copies ran while one was open for 30% of the time, Pallas kernels for 0%

commit v1 on v0

v1 whole, which is shorter than its diff:
```python
import jax
import jax.numpy as jnp
from jax import lax
from jax.experimental import pallas as pl
from jax.experimental.pallas import tpu as pltpu
from jax.sharding import PartitionSpec as P

BS = 128
F = 256
ROWS = 8
COLS = 32
HALF = 16
SLOTS = 8
WROWS = F // ROWS
SEND = F + WROWS
ANY = pl.BlockSpec(memory_space=pl.ANY)
VM = pl.BlockSpec(memory_space=pltpu.VMEM)
SM = pl.BlockSpec(memory_space=pltpu.SMEM)


def params(mb):
    return pltpu.CompilerParams(vmem_limit_bytes=mb * 1024 * 1024)


def masked(code_ref, v_ref, j, g):
    rows = []
    for k in range(SLOTS):
        code = code_ref[g * SLOTS + k]
        value = v_ref[j, k]
        left = jnp.where(code == 0, 1.0, 0.0).astype(jnp.bfloat16)
        right = jnp.where(code == 1, 1.0, 0.0).astype(jnp.bfloat16)
        rows.append(jnp.concatenate([value * left, value * right], axis=1))
    return jnp.concatenate(rows, axis=0)


def value_copy(ids, v_hbm, vbuf, vsem, j):
    return pltpu.make_async_copy(v_hbm.at[ids[j]], vbuf.at[j], vsem.at[j])


def forward_kernel(ids, code, dst, xa, xb, v_hbm, out, vbuf, xbuf, acc, vsem, xsem):
    def x_copy(j):
        ref = xa if j < HALF else xb
        return pltpu.make_async_copy(ref.at[j % HALF], xbuf.at[j], xsem.at[j])

    for j in range(COLS):
        value_copy(ids, v_hbm, vbuf, vsem, j).start()
        x_copy(j).start()
    acc[...] = jnp.zeros_like(acc)

    def step(j, _):
        value_copy(ids, v_hbm, vbuf, vsem, j).wait()
        pltpu.make_async_copy(xa.at[0], xbuf.at[j], xsem.at[j]).wait()
        g = ids[j]
        products = jnp.dot(masked(code, vbuf, j, g), xbuf[j], preferred_element_type=jnp.float32)
        for k in range(SLOTS):
            t = dst[g * SLOTS + k]
            acc[t] = acc[t] + products[k * BS : (k + 1) * BS]
        return 0

    lax.fori_loop(0, COLS, step, 0)
    for t in range(2 * ROWS):
        out[t] = acc[t].astype(jnp.bfloat16)


def middle_kernel(recv, weight, cot, act, send):
    total = recv[0].astype(jnp.float32)
    for r in range(1, ROWS):
        total = total + recv[r].astype(jnp.float32)
    aggregate = total.astype(jnp.bfloat16)
    w = weight[...]
    preact = jnp.dot(aggregate, w, preferred_element_type=jnp.float32)
    gate = jax.nn.sigmoid(preact)
    act[...] = (preact * gate).astype(jnp.bfloat16)
    delta = (cot[...].astype(jnp.float32) * gate * (1.0 + preact * (1.0 - gate))).astype(jnp.bfloat16)
    back_t = lax.dot_general(w, delta, (((1,), (1,)), ((), ())), preferred_element_type=jnp.float32)
    back_t = back_t.astype(jnp.bfloat16)
    local = lax.dot_general(aggregate, delta, (((0,), (0,)), ((), ())), preferred_element_type=jnp.float32)
    local = local.astype(jnp.bfloat16)
    for r in range(ROWS):
        send[r, :F] = back_t
        send[r, F:] = local[r * WROWS : (r + 1) * WROWS]


def backward_kernel(ids, code, dst, recv, v_hbm, mine, other, wsum, vbuf, bbuf, obuf, vsem, osem):
    for j in range(COLS):
        value_copy(ids, v_hbm, vbuf, vsem, j).start()
    total = recv[0, F:].astype(jnp.float32)
    for r in range(1, ROWS):
        total = total + recv[r, F:].astype(jnp.float32)
    wsum[...] = total
    for r in range(ROWS):
        for b in range(2):
            bbuf[2 * r + b] = recv[r, :F, b * BS : (b + 1) * BS]

    def step(j, _):
        value_copy(ids, v_hbm, vbuf, vsem, j).wait()
        g = ids[j]
        cat = jnp.concatenate([bbuf[dst[g * SLOTS + k]] for k in range(SLOTS)], axis=1)
        out = jnp.dot(cat, masked(code, vbuf, j, g), preferred_element_type=jnp.float32)
        obuf[j] = out.astype(jnp.bfloat16)
        return 0

    def run(ref, first):
        def one(i, _):
            step(first + i, 0)
            pltpu.make_async_copy(obuf.at[first + i], ref.at[i], osem.at[first + i]).start()
            return 0

        lax.fori_loop(0, HALF, one, 0)

    run(other, HALF)
    run(mine, 0)
    for j in range(COLS):
        ref = mine if j < HALF else other
        pltpu.make_async_copy(obuf.at[j], ref.at[j % HALF], osem.at[j]).wait()


def end_kernel(order, a, b, out):
    total = (a[...].astype(jnp.float32) + b[...].astype(jnp.float32)).T
    for q in range(2):
        out[order[q]] = total[q * BS : (q + 1) * BS].astype(jnp.bfloat16)


def col_perm(move):
    pairs = []
    for yl in range(2):
        for z in range(8):
            for core in range(2):
                to_yl, to_z, to_core = move(yl, z, core)
                pairs.append((yl * 16 + z * 2 + core, to_yl * 16 + to_z % 8 * 2 + to_core))
    return pairs


UP = col_perm(lambda yl, z, core: (yl, z + 1, core))
DOWN = col_perm(lambda yl, z, core: (yl, z - 1, core))
SWAP_Y = col_perm(lambda yl, z, core: (1 - yl, z, core))
SWAP_C = col_perm(lambda yl, z, core: (yl, z, 1 - core))


def send(a, perm):
    return lax.ppermute(a, "col", perm)


def gather_col(own):
    chains = []
    for first in (own, send(own, SWAP_Y)):
        pieces = {0: first}
        up = down = first
        for s in range(1, 5):
            up = send(up, UP)
            pieces[8 - s] = up
            if s < 4:
                down = send(down, DOWN)
                pieces[s] = down
        chains += [pieces[i] for i in range(8)]
    mine = jnp.concatenate(chains, axis=0)
    return mine.reshape(HALF, F, F), send(mine, SWAP_C).reshape(HALF, F, F)


def scatter_col(mine, other):
    got = send(other, SWAP_C)

    def part(j):
        return mine[j].astype(jnp.float32) + got[j].astype(jnp.float32)

    ends = []
    for y in (1, 0):
        base = y * 8
        up = part(base + 4).astype(jnp.bfloat16)
        down = part(base + 5).astype(jnp.bfloat16)
        for s in (3, 2, 1):
            up = send(up, UP)
            up = (part(base + s) + up.astype(jnp.float32)).astype(jnp.bfloat16)
            down = send(down, DOWN)
            if s > 1:
                down = (part(base + 9 - s) + down.astype(jnp.float32)).astype(jnp.bfloat16)
        up = send(up, UP)
        ends.append(part(base) + up.astype(jnp.float32) + down.astype(jnp.float32))
    far, near = ends
    return near.astype(jnp.bfloat16), send(far.astype(jnp.bfloat16), SWAP_Y)


def sum_weight(total):
    for perm in (
        SWAP_C,
        SWAP_Y,
        col_perm(lambda yl, z, core: (yl, z ^ 1, core)),
        col_perm(lambda yl, z, core: (yl, z ^ 2, core)),
        col_perm(lambda yl, z, core: (yl, z ^ 4, core)),
    ):
        total = total + send(total, perm)
    rows = (total * (1.0 / 256.0)).astype(jnp.bfloat16)
    return lax.all_gather(rows, "row", axis=0, tiled=True)


def body(features, weight, cotangent, block_values, source_block, target_block, block_counts, block_order):
    me = lax.axis_index("col")
    place = jnp.arange(COLS, dtype=jnp.int32)
    yl = (me // 16) ^ (place // 8 % 2)
    z = (me // 2 + place) % 8
    core = (me % 2) ^ (place // 16)
    ids = (yl * 16 + z * 2 + core).astype(jnp.int32)
    live = jnp.arange(SLOTS, dtype=jnp.int32)[None, :] < block_counts[0, 0][:, None]
    code = jnp.where(live, source_block[0, 0], 2).reshape(-1)
    dst = target_block[0, 0].reshape(-1)
    values = block_values[0, 0]
    order = block_order[0]

    swapped = jnp.concatenate([features[BS:], features[:BS]], axis=0)
    ordered = jnp.where(order[0] == 0, features, swapped)
    xa, xb = gather_col(ordered)

    value_scratch = [pltpu.VMEM((COLS, SLOTS, BS, BS), jnp.bfloat16)]
    partial = pl.pallas_call(
        forward_kernel,
        out_shape=jax.ShapeDtypeStruct((2 * ROWS, BS, F), jnp.bfloat16),
        in_specs=[SM, SM, SM, ANY, ANY, ANY],
        out_specs=VM,
        scratch_shapes=value_scratch
        + [
            pltpu.VMEM((COLS, F, F), jnp.bfloat16),
            pltpu.VMEM((2 * ROWS, BS, F), jnp.float32),
            pltpu.SemaphoreType.DMA((COLS,)),
            pltpu.SemaphoreType.DMA((COLS,)),
        ],
        compiler_params=params(48),
        name="forward",
    )(ids, code, dst, xa, xb, values)
    received = lax.all_to_all(partial.reshape(ROWS * F, F), "row", 0, 0, tiled=True)

    activated, outgoing = pl.pallas_call(
        middle_kernel,
        out_shape=(
            jax.ShapeDtypeStruct((F, F), jnp.bfloat16),
            jax.ShapeDtypeStruct((ROWS, SEND, F), jnp.bfloat16),
        ),
        in_specs=[VM, VM, VM],
        out_specs=(VM, VM),
        compiler_params=params(32),
        name="middle",
    )(received.reshape(ROWS, F, F), weight, cotangent)
    backs = lax.all_to_all(outgoing.reshape(ROWS * SEND, F), "row", 0, 0, tiled=True)

    mine, other, wsum = pl.pallas_call(
        backward_kernel,
        out_shape=(
            jax.ShapeDtypeStruct((HALF, F, F), jnp.bfloat16),
            jax.ShapeDtypeStruct((HALF, F, F), jnp.bfloat16),
            jax.ShapeDtypeStruct((WROWS, F), jnp.float32),
        ),
        in_specs=[SM, SM, SM, VM, ANY],
        out_specs=(ANY, ANY, VM),
        scratch_shapes=value_scratch
        + [
            pltpu.VMEM((2 * ROWS, F, BS), jnp.bfloat16),
            pltpu.VMEM((COLS, F, F), jnp.bfloat16),
            pltpu.SemaphoreType.DMA((COLS,)),
            pltpu.SemaphoreType.DMA((COLS,)),
        ],
        compiler_params=params(48),
        name="backward",
    )(ids, code, dst, backs.reshape(ROWS, SEND, F), values)

    near, far = scatter_col(mine, other)
    weight_grad = sum_weight(wsum)
    input_grad = pl.pallas_call(
        end_kernel,
        out_shape=jax.ShapeDtypeStruct((2, BS, F), jnp.bfloat16),
        in_specs=[SM, VM, VM],
        out_specs=VM,
        compiler_params=params(32),
        name="end",
    )(order, near, far)
    return activated, input_grad.reshape(F, F), weight_grad


def solution(mesh):
    in_specs = (
        P(("row", "col"), None),
        P(),
        P(("row", "col"), None),
        P("row", "col", None, None, None, None),
        P("row", "col", None, None),
        P("row", "col", None, None),
        P("row", "col", None),
        P(("row", "col"), None),
    )
    out_specs = (P(("row", "col"), None), P(("row", "col"), None), P())
    return jax.shard_map(body, mesh=mesh, in_specs=in_specs, out_specs=out_specs, check_vma=False)
```

time: 750 us -> 235 us (0.31)
  waiting for transfers between devices: 327 us -> 66.2 us
  matrix products: 235 us -> 0 us
  local copies, waits for them, and re-layouts: 82.3 us -> 2.16 us
  blocking collectives: 0 us -> 75.4 us
  loops' own time: 63.5 us -> 0 us
  starting transfers between devices: 0.2 us -> 47.8 us
  Pallas kernels: 0 us -> 37.2 us
  other arithmetic: 23 us -> 0.99 us
  between operations: 13.9 us -> 1.71 us
    dot_general x125 -> x0, matrix products: 235 us -> none  [the longest x32 60.6 us: backward_group(): jnp.einsum('kt,tjf->kjf', pick_hot, gathered, preferred_element_type=jnp....]
    reduce_scatter x2 -> x0, waiting for transfers between devices: 207 us -> none  [the longest x1 128 us: body(): lax.psum_scatter(lax.map(backward_group, group_list).reshape(lax.axis_siz...]
    all_gather x2 -> x0, waiting for transfers between devices: 120 us -> none  [the longest x1 70.2 us: body(): stripe = lax.all_gather(ordered, 'col', axis=0, tiled=True)]
    ppermute x0 -> x37, waiting for transfers between devices: none -> 66.2 us  [send(): return lax.ppermute(a, 'col', perm)]
    another operation x2 -> x0, loops' own time: 63.5 us -> none  [the longest x1 63.1 us: body(): lax.map(backward_group, group_list)]
    dynamic_slice x104 -> x0, local copies, waits for them, and re-layouts: 53.6 us -> none  [the longest x32 18.8 us: backward_group(): live_count = live_counts[group]]
    ppermute x0 -> x37, starting transfers between devices: none -> 47.8 us  [send(): return lax.ppermute(a, 'col', perm)]
    all_to_all x0 -> x2, blocking collectives: none -> 43.3 us  [the longest x1 22.5 us: body(): lax.all_to_all(partial.reshape(ROWS * F, F), 'row', 0, 0, tiled=True)]
  transfers between devices with their start and end apart: 5 -> 37, of which waited for: 4 -> 23; matrix products, arithmetic and copies ran while one was open for 30% -> 0% of each run, Pallas kernels for 0% -> 0%
where the time goes in v1:
time: 235 us; the launch traced here: 232 us
  blocking collectives  75.4 us (32%)
  waiting for transfers between devices  66.2 us (28%)
  starting transfers between devices  47.8 us (20%)
  Pallas kernels  37.2 us (16%)
    ppermute x37, waiting for transfers between devices, send(): return lax.ppermute(a, 'col', perm)  66.2 us
    ppermute x37, starting transfers between devices, send(): return lax.ppermute(a, 'col', perm)  47.8 us
    all_gather x1, blocking collectives, sum_weight(): return lax.all_gather(rows, 'row', axis=0, tiled=True)  32.1 us
    all_to_all x1, blocking collectives, body(): lax.all_to_all(partial.reshape(ROWS * F, F), 'row', 0, 0, tiled=True)  22.5 us
    all_to_all x1, blocking collectives, body(): lax.all_to_all(outgoing.reshape(ROWS * SEND, F), 'row', 0, 0, tiled=True)  20.8 us
    pallas_call x1, Pallas kernels, body(): pl.pallas_call(backward_kernel, out_shape=(jax.ShapeDtypeStruct((HALF, F,...  19.4 us
    pallas_call x1, Pallas kernels, body(): pl.pallas_call(forward_kernel, out_shape=jax.ShapeDtypeStruct((2 * ROWS,...  15.5 us
  transfers between devices with their start and end apart: 37, of which 23 were waited for; matrix products, arithmetic and copies ran while one was open for 0% of the time, Pallas kernels for 0%

profile of v1, /device:TPU:4, one launch (start us, length us, event | category | flops | bytes accessed | tf_op | source)
XLA Modules:
  0.0 231.5 jit_solution(2378073202941786330)
XLA Ops:
  4.3 4.9 %collective-permute-start = (bf16[256,256]{1,0:T(8,128)(2,1)S(1)}, bf16[256,256]{1,0:T(8,128)(2,1)S(1)}, u32[]{:S(2)}, u32[]{:S(2)}) collective-permute-start(bf16[256,256]{1,0:T(8,128)(2,1)S(1)} %get-tuple-element.14), channel_id=1, source_target_pairs={{0,14},{1,15},{2,0},{3,1},{4,2},{5,3},{6,4},{7,5},{8,6},{9,7},{10,... | collective-permute-start | bytes 393224 | tf_op jit(solution)/shard_map/ppermute | solution.py:141
  12.0 3.3 %collective-permute-start.1 = (bf16[256,256]{1,0:T(8,128)(2,1)S(1)}, bf16[256,256]{1,0:T(8,128)(2,1)S(1)}, u32[]{:S(2)}, u32[]{:S(2)}) collective-permute-start(bf16[256,256]{1,0:T(8,128)(2,1)S(1)} %collective-permute-done), channel_id=1, source_target_pairs={{0,14},{1,15},{2,0},{3,1},{4,2},{5,3},{6,4},{7,5},{8,6},{9,7},{10,... | collective-permute-start | bytes 393224 | tf_op jit(solution)/shard_map/ppermute | solution.py:141
  19.3 3.2 %collective-permute-start.2 = (bf16[256,256]{1,0:T(8,128)(2,1)S(1)}, bf16[256,256]{1,0:T(8,128)(2,1)S(1)}, u32[]{:S(2)}, u32[]{:S(2)}) collective-permute-start(bf16[256,256]{1,0:T(8,128)(2,1)S(1)} %collective-permute-done.1), channel_id=1, source_target_pairs={{0,14},{1,15},{2,0},{3,1},{4,2},{5,3},{6,4},{7,5},{8,6},{9,7},{10,... | collective-permute-start | bytes 393224 | tf_op jit(solution)/shard_map/ppermute | solution.py:141
  27.5 3.3 %collective-permute-start.10 = (bf16[256,256]{1,0:T(8,128)(2,1)S(1)}, bf16[256,256]{1,0:T(8,128)(2,1)S(1)}, u32[]{:S(2)}, u32[]{:S(2)}) collective-permute-start(bf16[256,256]{1,0:T(8,128)(2,1)S(1)} %collective-permute-done.9), channel_id=1, source_target_pairs={{0,14},{1,15},{2,0},{3,1},{4,2},{5,3},{6,4},{7,5},{8,6},{9,7},{10,... | collective-permute-start | bytes 393224 | tf_op jit(solution)/shard_map/ppermute | solution.py:141
  33.1 4.7 %collective-permute-done.13 = bf16[256,256]{1,0:T(8,128)(2,1)S(1)} collective-permute-done((bf16[256,256]{1,0:T(8,128)(2,1)S(1)}, bf16[256,256]{1,0:T(8,128)(2,1)S(1)}, u32[]{:S(2)}, u32[]{:S(2)}) %collective-permute-start.13) | collective-permute-done | bytes 131104 | tf_op jit(solution)/shard_map/ppermute | solution.py:141
  37.9 6.1 %collective-permute-done.14 = bf16[256,256]{1,0:T(8,128)(2,1)S(1)} collective-permute-done((bf16[256,256]{1,0:T(8,128)(2,1)S(1)}, bf16[256,256]{1,0:T(8,128)(2,1)S(1)}, u32[]{:S(2)}, u32[]{:S(2)}) %collective-permute-start.14) | collective-permute-done | bytes 131104 | tf_op jit(solution)/shard_map/ppermute | solution.py:141
  45.0 3.7 %collective-permute-done.15 = bf16[4096,256]{1,0:T(8,128)(2,1)} collective-permute-done((bf16[4096,256]{1,0:T(8,128)(2,1)S(1)}, bf16[4096,256]{1,0:T(8,128)(2,1)}, u32[]{:S(2)}, u32[]{:S(2)}) %collective-permute-start.15) | collective-permute-done | bytes 2097184 | tf_op jit(solution)/shard_map/ppermute | solution.py:141
  48.7 15.5 %forward.1 = bf16[16,128,256]{2,1,0:T(8,128)(2,1)S(1)} custom-call(s32[32]{0:T(128)S(1)} %fusion.19.ids, s32[256]{0:T(256)S(1)} %broadcast_select_fusion.code, s32[256]{0:T(256)S(1)} %reshape_squeeze.3.dst, bf16[16,256,256]{2,1,0:T(8,128)(2,1)S(1)} %bitcast.74, bf16[16,256,256]{2,1,0:T(8,128)(2,1)} %bitcast.3.xb, bf16[32,8,128,128]{3,2,1,0:T(8,128)(2,1)} %bitcast.77), custom_call_target="tpu_custom_call" | custom-call | tf_op jit(solution)/shard_map/forward/pallas_call | solution.py:214
  64.2 22.5 %all_to_all.15.recv = bf16[8,256,256]{2,1,0:T(8,128)(2,1)S(1)} all-to-all(bf16[8,256,256]{2,1,0:T(8,128)(2,1)S(1)} %bitcast.73), channel_id=1, replica_groups=mesh['row'=8,'col'=32] {'row'}, dimensions={0} | all-to-all | bytes 2097152 | tf_op jit(solution)/shard_map/all_to_all | solution.py:229
  87.7 20.8 %all_to_all.16.recv = bf16[8,288,256]{2,1,0:T(8,128)(2,1)S(1)} all-to-all(bf16[8,288,256]{2,1,0:T(8,128)(2,1)S(1)} %get-tuple-element.9), channel_id=1, replica_groups=mesh['row'=8,'col'=32] {'row'}, dimensions={0} | all-to-all | bytes 2359296 | tf_op jit(solution)/shard_map/all_to_all | solution.py:242
  108.5 19.4 %backward.1 = (bf16[16,256,256]{2,1,0:T(8,128)(2,1)S(1)}, bf16[16,256,256]{2,1,0:T(8,128)(2,1)S(1)}, f32[32,256]{1,0:T(8,128)S(1)}) custom-call(s32[32]{0:T(128)S(1)} %fusion.19.ids, s32[256]{0:T(256)S(1)} %broadcast_select_fusion.code, s32[256]{0:T(256)S(1)} %reshape_squeeze.3.dst, bf16[8,288,256]{2,1,0:T(8,128)(2,1)S(1)} %all_to_all.16.recv, ...), custom_call_target="tpu_custom_call" | custom-call | tf_op jit(solution)/shard_map/backward/pallas_call | solution.py:244
  128.0 4.1 %collective-permute-done.16 = bf16[16,256,256]{2,1,0:T(8,128)(2,1)S(1)} collective-permute-done((bf16[16,256,256]{2,1,0:T(8,128)(2,1)S(1)}, bf16[16,256,256]{2,1,0:T(8,128)(2,1)S(1)}, u32[]{:S(2)}, u32[]{:S(2)}) %collective-permute-start.16) | collective-permute-done | bytes 2097184 | tf_op jit(solution)/shard_map/ppermute | solution.py:141
  132.4 6.7 %collective-permute-done.24 = bf16[256,256]{1,0:T(8,128)(2,1)S(1)} collective-permute-done((bf16[256,256]{1,0:T(8,128)(2,1)S(1)}, bf16[256,256]{1,0:T(8,128)(2,1)S(1)}, u32[]{:S(2)}, u32[]{:S(2)}) %collective-permute-start.24) | collective-permute-done | bytes 131104 | tf_op jit(solution)/shard_map/ppermute | solution.py:141
  139.3 3.2 %collective-permute-start.28 = (bf16[256,256]{1,0:T(8,128)(2,1)S(1)}, bf16[256,256]{1,0:T(8,128)(2,1)S(1)}, u32[]{:S(2)}, u32[]{:S(2)}) collective-permute-start(bf16[256,256]{1,0:T(8,128)(2,1)S(1)} %get-tuple-element.21), channel_id=1, source_target_pairs={{0,14},{1,15},{2,0},{3,1},{4,2},{5,3},{6,4},{7,5},{8,6},{9,7},{10,... | collective-permute-start | bytes 393224 | tf_op jit(solution)/shard_map/ppermute | solution.py:141
  142.5 2.9 %collective-permute-done.25 = bf16[256,256]{1,0:T(8,128)(2,1)S(1)} collective-permute-done((bf16[256,256]{1,0:T(8,128)(2,1)S(1)}, bf16[256,256]{1,0:T(8,128)(2,1)S(1)}, u32[]{:S(2)}, u32[]{:S(2)}) %collective-permute-start.25) | collective-permute-done | bytes 131104 | tf_op jit(solution)/shard_map/ppermute | solution.py:141
  145.6 6.2 %collective-permute-done.26 = bf16[256,256]{1,0:T(8,128)(2,1)S(1)} collective-permute-done((bf16[256,256]{1,0:T(8,128)(2,1)S(1)}, bf16[256,256]{1,0:T(8,128)(2,1)S(1)}, u32[]{:S(2)}, u32[]{:S(2)}) %collective-permute-start.26) | collective-permute-done | bytes 131104 | tf_op jit(solution)/shard_map/ppermute | solution.py:141
  160.3 3.2 %collective-permute-done.30 = bf16[256,256]{1,0:T(8,128)(2,1)S(1)} collective-permute-done((bf16[256,256]{1,0:T(8,128)(2,1)S(1)}, bf16[256,256]{1,0:T(8,128)(2,1)S(1)}, u32[]{:S(2)}, u32[]{:S(2)}) %collective-permute-start.30) | collective-permute-done | bytes 131104 | tf_op jit(solution)/shard_map/ppermute | solution.py:141
  163.8 3.1 %collective-permute-start.22 = (bf16[256,256]{1,0:T(8,128)(2,1)S(1)}, bf16[256,256]{1,0:T(8,128)(2,1)S(1)}, u32[]{:S(2)}, u32[]{:S(2)}) collective-permute-start(bf16[256,256]{1,0:T(8,128)(2,1)S(1)} %get-tuple-element.16), channel_id=1, source_target_pairs={{0,14},{1,15},{2,0},{3,1},{4,2},{5,3},{6,4},{7,5},{8,6},{9,7},{10,... | collective-permute-start | bytes 393224 | tf_op jit(solution)/shard_map/ppermute | solution.py:141
  171.1 3.0 %collective-permute-done.33 = f32[32,256]{1,0:T(8,128)S(1)} collective-permute-done((f32[32,256]{1,0:T(8,128)S(1)}, f32[32,256]{1,0:T(8,128)S(1)}, u32[]{:S(2)}, u32[]{:S(2)}) %collective-permute-start.33) | collective-permute-done | bytes 32800 | tf_op jit(solution)/shard_map/ppermute | solution.py:141
  178.0 4.3 %collective-permute-start.35 = (f32[32,256]{1,0:T(8,128)S(1)}, f32[32,256]{1,0:T(8,128)S(1)}, u32[]{:S(2)}, u32[]{:S(2)}) collective-permute-start(f32[32,256]{1,0:T(8,128)S(1)} %add.226), channel_id=1, source_target_pairs={{0,4},{1,5},{2,6},{3,7},{4,0},{5,1},{6,2},{7,3},{8,12},{9,13},{10,... | collective-permute-start | bytes 98312 | tf_op jit(solution)/shard_map/ppermute | solution.py:141
  184.6 3.5 %collective-permute-start.36 = (f32[32,256]{1,0:T(8,128)S(1)}, f32[32,256]{1,0:T(8,128)S(1)}, u32[]{:S(2)}, u32[]{:S(2)}) collective-permute-start(f32[32,256]{1,0:T(8,128)S(1)} %add.227), channel_id=1, source_target_pairs={{0,8},{1,9},{2,10},{3,11},{4,12},{5,13},{6,14},{7,15},{8,0},{9,1},... | collective-permute-start | bytes 98312 | tf_op jit(solution)/shard_map/ppermute | solution.py:141
  188.3 3.6 %collective-permute-start.23 = (bf16[256,256]{1,0:T(8,128)(2,1)S(1)}, bf16[256,256]{1,0:T(8,128)(2,1)S(1)}, u32[]{:S(2)}, u32[]{:S(2)}) collective-permute-start(bf16[256,256]{1,0:T(8,128)(2,1)S(1)} %get-tuple-element.25), channel_id=1, source_target_pairs={{0,14},{1,15},{2,0},{3,1},{4,2},{5,3},{6,4},{7,5},{8,6},{9,7},{10,... | collective-permute-start | bytes 393224 | tf_op jit(solution)/shard_map/ppermute | solution.py:141
  192.5 32.1 %all_gather.3 = bf16[256,256]{1,0:T(8,128)(2,1)S(1)} all-gather(bf16[32,256]{1,0:T(8,128)(2,1)S(1)} %multiply_convert_fusion), channel_id=1, replica_groups=mesh['row'=8,'col'=32] {'row'}, dimensions={0}, use_global_device_ids=true | all-gather | bytes 147456 | tf_op jit(solution)/shard_map/all_gather | solution.py:193
  225.0 4.5 %collective-permute-done.31.b = bf16[256,256]{1,0:T(8,128)(2,1)S(1)} collective-permute-done((bf16[256,256]{1,0:T(8,128)(2,1)S(1)}, bf16[256,256]{1,0:T(8,128)(2,1)S(1)}, u32[]{:S(2)}, u32[]{:S(2)}) %collective-permute-start.31) | collective-permute-done | bytes 131104 | tf_op jit(solution)/shard_map/ppermute | solution.py:141
  (109 shorter events, 41.8 us)
Async XLA Ops:
  2.3 9.8 %collective-permute-start.3 = (bf16[256,256]{1,0:T(8,128)(2,1)S(1)}, bf16[256,256]{1,0:T(8,128)(2,1)S(1)}, u32[]{:S(2)}, u32[]{:S(2)}) collective-permute-start(bf16[256,256]{1,0:T(8,128)(2,1)S(1)} %get-tuple-element.14), channel_id=1, source_target_pairs={{0,2},{1,3},{2,4},{3,5},{4,6},{5,7},{6,8},{7,9},{8,10},{9,11},{10,... | collective-permute-start | bytes 393224 | tf_op jit(solution)/shard_map/ppermute | solution.py:141
  4.3 7.8 %collective-permute-start = (bf16[256,256]{1,0:T(8,128)(2,1)S(1)}, bf16[256,256]{1,0:T(8,128)(2,1)S(1)}, u32[]{:S(2)}, u32[]{:S(2)}) collective-permute-start(bf16[256,256]{1,0:T(8,128)(2,1)S(1)} %get-tuple-element.14), channel_id=1, source_target_pairs={{0,14},{1,15},{2,0},{3,1},{4,2},{5,3},{6,4},{7,5},{8,6},{9,7},{10,... | collective-permute-start | bytes 393224 | tf_op jit(solution)/shard_map/ppermute | solution.py:141
  12.0 7.3 %collective-permute-start.4 = (bf16[256,256]{1,0:T(8,128)(2,1)S(1)}, bf16[256,256]{1,0:T(8,128)(2,1)S(1)}, u32[]{:S(2)}, u32[]{:S(2)}) collective-permute-start(bf16[256,256]{1,0:T(8,128)(2,1)S(1)} %collective-permute-done.3), channel_id=1, source_target_pairs={{0,2},{1,3},{2,4},{3,5},{4,6},{5,7},{6,8},{7,9},{8,10},{9,11},{10,... | collective-permute-start | bytes 393224 | tf_op jit(solution)/shard_map/ppermute | solution.py:141
  12.0 7.3 %collective-permute-start.1 = (bf16[256,256]{1,0:T(8,128)(2,1)S(1)}, bf16[256,256]{1,0:T(8,128)(2,1)S(1)}, u32[]{:S(2)}, u32[]{:S(2)}) collective-permute-start(bf16[256,256]{1,0:T(8,128)(2,1)S(1)} %collective-permute-done), channel_id=1, source_target_pairs={{0,14},{1,15},{2,0},{3,1},{4,2},{5,3},{6,4},{7,5},{8,6},{9,7},{10,... | collective-permute-start | bytes 393224 | tf_op jit(solution)/shard_map/ppermute | solution.py:141
  15.4 7.2 %collective-permute-start.8 = (bf16[256,256]{1,0:T(8,128)(2,1)S(1)}, bf16[256,256]{1,0:T(8,128)(2,1)S(1)}, u32[]{:S(2)}, u32[]{:S(2)}) collective-permute-start(bf16[256,256]{1,0:T(8,128)(2,1)S(1)} %collective-permute-done.7), channel_id=1, source_target_pairs={{0,14},{1,15},{2,0},{3,1},{4,2},{5,3},{6,4},{7,5},{8,6},{9,7},{10,... | collective-permute-start | bytes 393224 | tf_op jit(solution)/shard_map/ppermute | solution.py:141
  16.1 7.7 %collective-permute-start.11 = (bf16[256,256]{1,0:T(8,128)(2,1)S(1)}, bf16[256,256]{1,0:T(8,128)(2,1)S(1)}, u32[]{:S(2)}, u32[]{:S(2)}) collective-permute-start(bf16[256,256]{1,0:T(8,128)(2,1)S(1)} %collective-permute-done.7), channel_id=1, source_target_pairs={{0,2},{1,3},{2,4},{3,5},{4,6},{5,7},{6,8},{7,9},{8,10},{9,11},{10,... | collective-permute-start | bytes 393224 | tf_op jit(solution)/shard_map/ppermute | solution.py:141
  19.3 7.6 %collective-permute-start.5 = (bf16[256,256]{1,0:T(8,128)(2,1)S(1)}, bf16[256,256]{1,0:T(8,128)(2,1)S(1)}, u32[]{:S(2)}, u32[]{:S(2)}) collective-permute-start(bf16[256,256]{1,0:T(8,128)(2,1)S(1)} %collective-permute-done.4), channel_id=1, source_target_pairs={{0,2},{1,3},{2,4},{3,5},{4,6},{5,7},{6,8},{7,9},{8,10},{9,11},{10,... | collective-permute-start | bytes 393224 | tf_op jit(solution)/shard_map/ppermute | solution.py:141
  19.3 11.6 %collective-permute-start.2 = (bf16[256,256]{1,0:T(8,128)(2,1)S(1)}, bf16[256,256]{1,0:T(8,128)(2,1)S(1)}, u32[]{:S(2)}, u32[]{:S(2)}) collective-permute-start(bf16[256,256]{1,0:T(8,128)(2,1)S(1)} %collective-permute-done.1), channel_id=1, source_target_pairs={{0,14},{1,15},{2,0},{3,1},{4,2},{5,3},{6,4},{7,5},{8,6},{9,7},{10,... | collective-permute-start | bytes 393224 | tf_op jit(solution)/shard_map/ppermute | solution.py:141
  23.8 7.1 %collective-permute-start.12 = (bf16[256,256]{1,0:T(8,128)(2,1)S(1)}, bf16[256,256]{1,0:T(8,128)(2,1)S(1)}, u32[]{:S(2)}, u32[]{:S(2)}) collective-permute-start(bf16[256,256]{1,0:T(8,128)(2,1)S(1)} %collective-permute-done.11), channel_id=1, source_target_pairs={{0,2},{1,3},{2,4},{3,5},{4,6},{5,7},{6,8},{7,9},{8,10},{9,11},{10,... | collective-permute-start | bytes 393224 | tf_op jit(solution)/shard_map/ppermute | solution.py:141
  27.5 10.4 %collective-permute-start.10 = (bf16[256,256]{1,0:T(8,128)(2,1)S(1)}, bf16[256,256]{1,0:T(8,128)(2,1)S(1)}, u32[]{:S(2)}, u32[]{:S(2)}) collective-permute-start(bf16[256,256]{1,0:T(8,128)(2,1)S(1)} %collective-permute-done.9), channel_id=1, source_target_pairs={{0,14},{1,15},{2,0},{3,1},{4,2},{5,3},{6,4},{7,5},{8,6},{9,7},{10,... | collective-permute-start | bytes 393224 | tf_op jit(solution)/shard_map/ppermute | solution.py:141
  30.9 6.9 %collective-permute-start.13 = (bf16[256,256]{1,0:T(8,128)(2,1)S(1)}, bf16[256,256]{1,0:T(8,128)(2,1)S(1)}, u32[]{:S(2)}, u32[]{:S(2)}) collective-permute-start(bf16[256,256]{1,0:T(8,128)(2,1)S(1)} %collective-permute-done.12), channel_id=1, source_target_pairs={{0,2},{1,3},{2,4},{3,5},{4,6},{5,7},{6,8},{7,9},{8,10},{9,11},{10,... | collective-permute-start | bytes 393224 | tf_op jit(solution)/shard_map/ppermute | solution.py:141
  132.3 6.8 %collective-permute-start.24 = (bf16[256,256]{1,0:T(8,128)(2,1)S(1)}, bf16[256,256]{1,0:T(8,128)(2,1)S(1)}, u32[]{:S(2)}, u32[]{:S(2)}) collective-permute-start(bf16[256,256]{1,0:T(8,128)(2,1)S(1)} %get-tuple-element.20), channel_id=1, source_target_pairs={{0,2},{1,3},{2,4},{3,5},{4,6},{5,7},{6,8},{7,9},{8,10},{9,11},{10,... | collective-permute-start | bytes 393224 | tf_op jit(solution)/shard_map/ppermute | solution.py:141
  139.3 6.3 %collective-permute-start.28 = (bf16[256,256]{1,0:T(8,128)(2,1)S(1)}, bf16[256,256]{1,0:T(8,128)(2,1)S(1)}, u32[]{:S(2)}, u32[]{:S(2)}) collective-permute-start(bf16[256,256]{1,0:T(8,128)(2,1)S(1)} %get-tuple-element.21), channel_id=1, source_target_pairs={{0,14},{1,15},{2,0},{3,1},{4,2},{5,3},{6,4},{7,5},{8,6},{9,7},{10,... | collective-permute-start | bytes 393224 | tf_op jit(solution)/shard_map/ppermute | solution.py:141
  145.5 6.3 %collective-permute-start.26 = (bf16[256,256]{1,0:T(8,128)(2,1)S(1)}, bf16[256,256]{1,0:T(8,128)(2,1)S(1)}, u32[]{:S(2)}, u32[]{:S(2)}) collective-permute-start(bf16[256,256]{1,0:T(8,128)(2,1)S(1)} %fusion.3), channel_id=1, source_target_pairs={{0,2},{1,3},{2,4},{3,5},{4,6},{5,7},{6,8},{7,9},{8,10},{9,11},{10,... | collective-permute-start | bytes 393224 | tf_op jit(solution)/shard_map/ppermute | solution.py:141
  151.9 6.4 %collective-permute-start.29 = (bf16[256,256]{1,0:T(8,128)(2,1)S(1)}, bf16[256,256]{1,0:T(8,128)(2,1)S(1)}, u32[]{:S(2)}, u32[]{:S(2)}) collective-permute-start(bf16[256,256]{1,0:T(8,128)(2,1)S(1)} %get-tuple-element.19), channel_id=1, source_target_pairs={{0,14},{1,15},{2,0},{3,1},{4,2},{5,3},{6,4},{7,5},{8,6},{9,7},{10,... | collective-permute-start | bytes 393224 | tf_op jit(solution)/shard_map/ppermute | solution.py:141
  152.0 7.8 %collective-permute-start.21 = (bf16[256,256]{1,0:T(8,128)(2,1)S(1)}, bf16[256,256]{1,0:T(8,128)(2,1)S(1)}, u32[]{:S(2)}, u32[]{:S(2)}) collective-permute-start(bf16[256,256]{1,0:T(8,128)(2,1)S(1)} %get-tuple-element.22), channel_id=1, source_target_pairs={{0,14},{1,15},{2,0},{3,1},{4,2},{5,3},{6,4},{7,5},{8,6},{9,7},{10,... | collective-permute-start | bytes 393224 | tf_op jit(solution)/shard_map/ppermute | solution.py:141
  152.4 7.3 %collective-permute-start.17 = (bf16[256,256]{1,0:T(8,128)(2,1)S(1)}, bf16[256,256]{1,0:T(8,128)(2,1)S(1)}, u32[]{:S(2)}, u32[]{:S(2)}) collective-permute-start(bf16[256,256]{1,0:T(8,128)(2,1)S(1)} %get-tuple-element.23), channel_id=1, source_target_pairs={{0,2},{1,3},{2,4},{3,5},{4,6},{5,7},{6,8},{7,9},{8,10},{9,11},{10,... | collective-permute-start | bytes 393224 | tf_op jit(solution)/shard_map/ppermute | solution.py:141
  163.7 6.3 %collective-permute-start.32 = (f32[32,256]{1,0:T(8,128)S(1)}, f32[32,256]{1,0:T(8,128)S(1)}, u32[]{:S(2)}, u32[]{:S(2)}) collective-permute-start(f32[32,256]{1,0:T(8,128)S(1)} %get-tuple-element.12), channel_id=1, source_target_pairs={{0,1},{1,0},{2,3},{3,2},{4,5},{5,4},{6,7},{7,6},{8,9},{9,8},{10,11... | collective-permute-start | bytes 98312 | tf_op jit(solution)/shard_map/ppermute | solution.py:141
  163.8 24.3 %collective-permute-start.22 = (bf16[256,256]{1,0:T(8,128)(2,1)S(1)}, bf16[256,256]{1,0:T(8,128)(2,1)S(1)}, u32[]{:S(2)}, u32[]{:S(2)}) collective-permute-start(bf16[256,256]{1,0:T(8,128)(2,1)S(1)} %get-tuple-element.16), channel_id=1, source_target_pairs={{0,14},{1,15},{2,0},{3,1},{4,2},{5,3},{6,4},{7,5},{8,6},{9,7},{10,... | collective-permute-start | bytes 393224 | tf_op jit(solution)/shard_map/ppermute | solution.py:141
  169.9 18.2 %collective-permute-start.19 = (bf16[256,256]{1,0:T(8,128)(2,1)S(1)}, bf16[256,256]{1,0:T(8,128)(2,1)S(1)}, u32[]{:S(2)}, u32[]{:S(2)}) collective-permute-start(bf16[256,256]{1,0:T(8,128)(2,1)S(1)} %fusion.10), channel_id=1, source_target_pairs={{0,2},{1,3},{2,4},{3,5},{4,6},{5,7},{6,8},{7,9},{8,10},{9,11},{10,... | collective-permute-start | bytes 393224 | tf_op jit(solution)/shard_map/ppermute | solution.py:141
  178.0 6.6 %collective-permute-start.35 = (f32[32,256]{1,0:T(8,128)S(1)}, f32[32,256]{1,0:T(8,128)S(1)}, u32[]{:S(2)}, u32[]{:S(2)}) collective-permute-start(f32[32,256]{1,0:T(8,128)S(1)} %add.226), channel_id=1, source_target_pairs={{0,4},{1,5},{2,6},{3,7},{4,0},{5,1},{6,2},{7,3},{8,12},{9,13},{10,... | collective-permute-start | bytes 98312 | tf_op jit(solution)/shard_map/ppermute | solution.py:141
  184.6 7.8 %collective-permute-start.36 = (f32[32,256]{1,0:T(8,128)S(1)}, f32[32,256]{1,0:T(8,128)S(1)}, u32[]{:S(2)}, u32[]{:S(2)}) collective-permute-start(f32[32,256]{1,0:T(8,128)S(1)} %add.227), channel_id=1, source_target_pairs={{0,8},{1,9},{2,10},{3,11},{4,12},{5,13},{6,14},{7,15},{8,0},{9,1},... | collective-permute-start | bytes 98312 | tf_op jit(solution)/shard_map/ppermute | solution.py:141
  188.3 36.7 %collective-permute-start.23 = (bf16[256,256]{1,0:T(8,128)(2,1)S(1)}, bf16[256,256]{1,0:T(8,128)(2,1)S(1)}, u32[]{:S(2)}, u32[]{:S(2)}) collective-permute-start(bf16[256,256]{1,0:T(8,128)(2,1)S(1)} %get-tuple-element.25), channel_id=1, source_target_pairs={{0,14},{1,15},{2,0},{3,1},{4,2},{5,3},{6,4},{7,5},{8,6},{9,7},{10,... | collective-permute-start | bytes 393224 | tf_op jit(solution)/shard_map/ppermute | solution.py:141
  191.8 33.1 %collective-permute-start.20 = (bf16[256,256]{1,0:T(8,128)(2,1)S(1)}, bf16[256,256]{1,0:T(8,128)(2,1)S(1)}, u32[]{:S(2)}, u32[]{:S(2)}) collective-permute-start(bf16[256,256]{1,0:T(8,128)(2,1)S(1)} %get-tuple-element.24), channel_id=1, source_target_pairs={{0,2},{1,3},{2,4},{3,5},{4,6},{5,7},{6,8},{7,9},{8,10},{9,11},{10,... | collective-permute-start | bytes 393224 | tf_op jit(solution)/shard_map/ppermute | solution.py:141
  (19 other events, 312.2 us)

commit v2 on v0

v2 whole, which is shorter than its diff:
```python
import functools

import jax
import jax.numpy as jnp
from jax import lax
from jax.experimental import pallas as pl
from jax.experimental.pallas import tpu as pltpu
from jax.sharding import PartitionSpec as P

BS = 128
F = 256
ROWS = 8
COLS = 32
SLOTS = 8
WROWS = F // ROWS
SEND = 2 * F + 2 * WROWS
HBM = pl.BlockSpec(memory_space=pltpu.HBM)
VM = pl.BlockSpec(memory_space=pltpu.VMEM)
SM = pl.BlockSpec(memory_space=pltpu.SMEM)
DISTANCES = (0, 7, 1, 6, 2, 5, 3, 4)
HALF = 16
OWN = 0
SIBLING = 16


def params(mb):
    return pltpu.CompilerParams(vmem_limit_bytes=mb * 1024 * 1024)


def cost(flops, moved):
    return pl.CostEstimate(flops=flops, bytes_accessed=moved, transcendentals=0)


def products(groups):
    return cost(2 * groups * SLOTS * BS * BS * F, groups * 1024 * 1024)


def forward_groups(first, ids, src, dst, x, values, acc):
    for j in range(x.shape[0]):
        g = ids[first + j]
        for k in range(SLOTS):
            s = src[g * SLOTS + k]
            t = dst[g * SLOTS + k]
            picked = x[j, pl.ds(pl.multiple_of(s * BS, BS), BS)]
            acc[t] = acc[t] + jnp.dot(values[g, k], picked, preferred_element_type=jnp.float32)


def stream(first, ids, values, vbuf, vsem):
    groups = vbuf.shape[0]
    ends = [2, *range(6, groups, 4), groups]

    def copy(j):
        return pltpu.make_async_copy(values.at[ids[first + j]], vbuf.at[j], vsem.at[j])

    for j in range(groups):
        copy(j).start()

    def ready(j):
        for begin, end in zip([0] + ends, ends):
            if j == begin:
                for i in range(begin, end):
                    copy(i).wait()

    return ready


def forward_groups(first, ids, src, dst, x, values, acc, vbuf, vsem, begin):
    ready = stream(first, ids, values, vbuf, vsem)
    begin()
    for j in range(x.shape[0]):
        ready(j)
        g = ids[first + j]
        for k in range(SLOTS):
            s = src[g * SLOTS + k]
            t = dst[g * SLOTS + k]
            picked = x[j, pl.ds(pl.multiple_of(s * BS, BS), BS)]
            acc[t] = acc[t] + jnp.dot(vbuf[j, k], picked, preferred_element_type=jnp.float32)


def forward_first(first, ids, src, dst, x, values, acc, vbuf, vsem):
    def begin():
        acc[...] = jnp.zeros_like(acc)

    forward_groups(first, ids, src, dst, x, values, acc, vbuf, vsem, begin)


def forward_last(first, ids, src, dst, x, values, begun, out, vbuf, vsem, acc):
    def begin():
        acc[...] = begun[...]

    forward_groups(first, ids, src, dst, x, values, acc, vbuf, vsem, begin)
    for t in range(2 * ROWS):
        out[t] = acc[t].astype(jnp.bfloat16)


def middle_kernel(recv, weight, cot, act, send):
    total = recv[0].astype(jnp.float32)
    for r in range(1, ROWS):
        total = total + recv[r].astype(jnp.float32)
    aggregate = total.astype(jnp.bfloat16)
    w = weight[...]
    preact = jnp.dot(aggregate, w, preferred_element_type=jnp.float32)
    gate = jax.nn.sigmoid(preact)
    act[...] = (preact * gate).astype(jnp.bfloat16)
    delta = (cot[...].astype(jnp.float32) * gate * (1.0 + preact * (1.0 - gate))).astype(jnp.bfloat16)
    back_t = lax.dot_general(w, delta, (((1,), (1,)), ((), ())), preferred_element_type=jnp.float32)
    back_t = back_t.astype(jnp.bfloat16)
    local = lax.dot_general(aggregate, delta, (((0,), (0,)), ((), ())), preferred_element_type=jnp.float32)
    local = local.astype(jnp.bfloat16)
    for r in range(ROWS):
        for b in range(2):
            half = slice(b * BS, (b + 1) * BS)
            send[r, b * F : (b + 1) * F] = back_t[:, half]
            at = 2 * F + b * WROWS
            send[r, at : at + WROWS] = local[r * WROWS : (r + 1) * WROWS, half]


def backward_kernel(first, ids, code, dst, recv, values, out, vbuf, vsem, acc):
    ready = stream(first, ids, values, vbuf, vsem)
    for j in range(out.shape[0]):
        ready(j)
        g = ids[first + j]
        acc[j] = jnp.zeros((3, F, BS), jnp.float32)
        for k in range(SLOTS):
            c = code[g * SLOTS + k]
            t = dst[g * SLOTS + k]
            picked = recv[t // 2, pl.ds(pl.multiple_of(t % 2 * F, F), F)]
            acc[j, c] = acc[j, c] + jnp.dot(picked, vbuf[j, k], preferred_element_type=jnp.float32)
        for q in range(2):
            out[j, q * F : (q + 1) * F] = acc[j, q].astype(jnp.bfloat16)


def end_kernel(order, a, b, out):
    total = a[...].astype(jnp.float32) + b[...].astype(jnp.float32)
    for q in range(2):
        out[order[q]] = total[q * F : (q + 1) * F].T.astype(jnp.bfloat16)


def sum_kernel(z, *refs):
    out, scratch = refs[ROWS], refs[ROWS + 1]
    for i, distance in enumerate((0, 7, 6, 5, 4, 1, 2, 3)):
        scratch[(z[0] + distance) % 8] = refs[i][...]
    total = scratch[0].astype(jnp.float32)
    for i in range(1, 8):
        total = total + scratch[i].astype(jnp.float32)
    out[...] = (total * (1.0 / 256.0)).astype(jnp.bfloat16)


def weight_kernel(me, *refs):
    out = refs[-1]
    for k in range(ROWS):
        rows = pl.ds(pl.multiple_of((me[0] ^ k) * WROWS, WROWS), WROWS)
        out[rows, :BS] = refs[k][:WROWS]
        out[rows, BS:] = refs[k][WROWS:]


def col_perm(move):
    pairs = []
    for yl in range(2):
        for z in range(8):
            for core in range(2):
                to_yl, to_z, to_core = move(yl, z, core)
                pairs.append((yl * 16 + z * 2 + core, to_yl * 16 + to_z % 8 * 2 + to_core))
    return pairs


UP = col_perm(lambda yl, z, core: (yl, z + 1, core))
DOWN = col_perm(lambda yl, z, core: (yl, z - 1, core))
SWAP_Y = col_perm(lambda yl, z, core: (1 - yl, z, core))
SWAP_C = col_perm(lambda yl, z, core: (yl, z, 1 - core))
Z1, Z2, Z4 = [col_perm(lambda yl, z, core, bit=bit: (yl, z ^ bit, core)) for bit in (1, 2, 4)]


def send(a, perm):
    return lax.ppermute(a, "col", perm)


def across(a, k):
    return lax.ppermute(a, "row", [(r, r ^ k) for r in range(ROWS)])


def together(*arrays):
    return lax.optimization_barrier(arrays)


def call(kernel, out_shape, specs, name, mb, scratch=(), estimate=None):
    out_specs = jax.tree.map(lambda _: VM, out_shape)
    return pl.pallas_call(
        kernel,
        out_shape=out_shape,
        in_specs=specs,
        out_specs=out_specs,
        scratch_shapes=list(scratch),
        compiler_params=params(mb),
        cost_estimate=estimate,
        name=name,
    )


def bf(a):
    return a.astype(jnp.bfloat16)


def f32(a):
    return a.astype(jnp.float32)


def cat(*arrays):
    return jnp.concatenate(arrays, axis=0)


def buffers(groups):
    return [pltpu.VMEM((groups, SLOTS, BS, BS), jnp.bfloat16), pltpu.SemaphoreType.DMA((groups,))]


def forward(features, order, tables, values):
    swapped = cat(features[BS:], features[:BS])
    own = jnp.where(order[0] == 0, features, swapped)
    totals = jax.ShapeDtypeStruct((2 * ROWS + 1, BS, F), jnp.float32)

    def run(kernel, name, first, x, *begun, out=totals, scratch=()):
        x = x.reshape(-1, F, F)
        specs = [SM] * 3 + [VM, HBM] + [VM] * len(begun)
        scratch = buffers(x.shape[0]) + list(scratch)
        return call(
            functools.partial(kernel, first), out, specs, name, 48, scratch=scratch, estimate=products(x.shape[0])
        )(*tables, x, values, *begun)

    (own,) = together(own)
    pair = cat(own, send(own, SWAP_Y))
    ups, downs = [pair], [pair]
    for _ in range(3):
        ups.append(send(ups[-1], UP))
        downs.append(send(downs[-1], DOWN))
    last = send(ups[3][:F], UP), send(downs[3][F:], DOWN)
    near = cat(pair, ups[1], downs[1], ups[2], downs[2], ups[3], downs[3], *last)
    far = send(near, SWAP_C)
    begun = run(forward_first, "forward_1", OWN, near)
    out = jax.ShapeDtypeStruct((2 * ROWS, BS, F), jnp.bfloat16)
    scratch = [pltpu.VMEM(totals.shape, jnp.float32)]
    return run(forward_last, "forward_2", SIBLING, far, begun, out=out, scratch=scratch)


def backward(backs, tables, values, z):
    def run(name, first, groups=HALF):
        return call(
            functools.partial(backward_kernel, first),
            jax.ShapeDtypeStruct((groups, 2 * F, BS), jnp.bfloat16),
            [SM] * 3 + [VM, HBM],
            name,
            48,
            scratch=buffers(groups) + [pltpu.VMEM((groups, 3, F, BS), jnp.float32)],
            estimate=products(groups),
        )(*tables, backs, values)

    def hop(total, piece, perm):
        got = send(cat(bf(total), piece), perm)
        n = got.shape[0] - 2 * WROWS
        return f32(got[:n]), got[n:]

    def part(mine, got, lo, hi):
        return (f32(mine[lo:hi]) + f32(got[lo:hi])).reshape(-1, BS)

    w = jnp.sum(f32(backs[:, 2 * F :]), axis=0)
    other, got_w = together(run("backward_1", SIBLING), send(w, SWAP_Y))
    w = w + got_w
    got, got_w = together(send(other, SWAP_C), send(w, SWAP_C))
    mine = run("backward_2", OWN)
    w = bf(w + got_w)
    def pair(i):
        return part(mine, got, 2 * i, 2 * i + 2)

    up, up1 = hop(part(mine, got, 14, 15), w, UP)
    down, down1 = hop(part(mine, got, 15, 16), w, DOWN)
    zero = jnp.zeros_like(up)
    up, up2 = hop(pair(6) + cat(up, zero), up1, UP)
    down, down2 = hop(pair(5) + cat(zero, down), down1, DOWN)
    opposite = send(w, Z4)
    up, up3 = hop(pair(4) + up, up2, UP)
    down, down3 = hop(pair(3) + down, down2, DOWN)
    up = f32(send(bf(pair(2) + up), UP))
    down = f32(send(bf(pair(1) + down), DOWN))
    own = bf(pair(0) + up + down)
    far = send(own[2 * F :], SWAP_Y)
    piece = jax.ShapeDtypeStruct((2 * WROWS, BS), jnp.bfloat16)
    scratch = [pltpu.VMEM((8, 2 * WROWS, BS), jnp.bfloat16)]
    w = call(sum_kernel, piece, [SM] + [VM] * 8, "sum", 8, scratch=scratch)(
        z, w, up1, up2, up3, opposite, down1, down2, down3
    )
    pairs = cat(w, across(w, 1))
    rows = [pairs] + [across(pairs, k) for k in (2, 4, 6)]
    return own[: 2 * F], far, [half for a in rows for half in (a[: 2 * WROWS], a[2 * WROWS :])]


def body(features, weight, cotangent, block_values, source_block, target_block, block_counts, block_order):
    me = lax.axis_index("col").astype(jnp.int32)
    place = jnp.arange(COLS, dtype=jnp.int32)
    distance = jnp.repeat(jnp.array(DISTANCES * 2, jnp.int32), 2)
    ids = ((me // 16) ^ (place % 2)) * 16 + (me // 2 + distance) % 8 * 2 + ((me % 2) ^ (place // SIBLING))
    live = jnp.arange(SLOTS, dtype=jnp.int32)[None, :] < block_counts[0, 0][:, None]
    live = live.reshape(-1)
    src = source_block[0, 0].reshape(-1)
    dst = target_block[0, 0].reshape(-1)
    values = block_values[0, 0]
    order = block_order[0]
    bf16 = jnp.bfloat16

    partial = forward(features, order, (ids, src, jnp.where(live, dst, 2 * ROWS)), values)
    received = lax.all_to_all(partial.reshape(ROWS * F, F), "row", 0, 0, tiled=True)
    piece = jax.ShapeDtypeStruct((F, F), bf16)
    activated, outgoing = call(
        middle_kernel, (piece, jax.ShapeDtypeStruct((ROWS, SEND, BS), bf16)), [VM, VM, VM], "middle", 8
    )(received.reshape(ROWS, F, F), weight, cotangent)
    backs = lax.all_to_all(outgoing.reshape(ROWS * SEND, BS), "row", 0, 0, tiled=True)
    backs = backs.reshape(ROWS, SEND, BS)

    z = (me // 2 % 8).reshape(1)
    a, b, rows = backward(backs, (ids, jnp.where(live, src, 2), dst), values, z)
    row = lax.axis_index("row").astype(jnp.int32).reshape(1)
    weight_grad = call(weight_kernel, piece, [SM] + [VM] * ROWS, "weight", 8)(row, *rows)
    input_grad = call(end_kernel, jax.ShapeDtypeStruct((2, BS, F), bf16), [SM, VM, VM], "end", 8)(order, a, b)
    return activated, input_grad.reshape(F, F), weight_grad


def solution(mesh):
    in_specs = (
        P(("row", "col"), None),
        P(),
        P(("row", "col"), None),
        P("row", "col", None, None, None, None),
        P("row", "col", None, None),
        P("row", "col", None, None),
        P("row", "col", None),
        P(("row", "col"), None),
    )
    out_specs = (P(("row", "col"), None), P(("row", "col"), None), P())
    return jax.shard_map(body, mesh=mesh, in_specs=in_specs, out_specs=out_specs, check_vma=False)
```

time: 750 us -> 163 us (0.22)
  waiting for transfers between devices: 327 us -> 47.3 us
  matrix products: 235 us -> 0 us
  local copies, waits for them, and re-layouts: 82.3 us -> 1.75 us
  loops' own time: 63.5 us -> 0 us
  blocking collectives: 0 us -> 43.3 us
  starting transfers between devices: 0.2 us -> 41.6 us
  Pallas kernels: 0 us -> 24.5 us
  other arithmetic: 23 us -> 1.18 us
  between operations: 13.9 us -> 1.86 us
    dot_general x125 -> x0, matrix products: 235 us -> none  [the longest x32 60.6 us: backward_group(): jnp.einsum('kt,tjf->kjf', pick_hot, gathered, preferred_element_type=jnp....]
    reduce_scatter x2 -> x0, waiting for transfers between devices: 207 us -> none  [the longest x1 128 us: body(): lax.psum_scatter(lax.map(backward_group, group_list).reshape(lax.axis_siz...]
    all_gather x2 -> x0, waiting for transfers between devices: 120 us -> none  [the longest x1 70.2 us: body(): stripe = lax.all_gather(ordered, 'col', axis=0, tiled=True)]
    another operation x2 -> x0, loops' own time: 63.5 us -> none  [the longest x1 63.1 us: body(): lax.map(backward_group, group_list)]
    dynamic_slice x104 -> x0, local copies, waits for them, and re-layouts: 53.6 us -> none  [the longest x32 18.8 us: backward_group(): live_count = live_counts[group]]
    ppermute x0 -> x27, waiting for transfers between devices: none -> 47.3 us  [the longest x23 41.6 us: send(): return lax.ppermute(a, 'col', perm)]
    all_to_all x0 -> x2, blocking collectives: none -> 43.3 us  [the longest x1 22.5 us: body(): lax.all_to_all(partial.reshape(ROWS * F, F), 'row', 0, 0, tiled=True)]
    ppermute x0 -> x27, starting transfers between devices: none -> 41.6 us  [the longest x23 37.1 us: send(): return lax.ppermute(a, 'col', perm)]
  transfers between devices with their start and end apart: 5 -> 27, of which waited for: 4 -> 13; matrix products, arithmetic and copies ran while one was open for 30% -> 1% of each run, Pallas kernels for 0% -> 10%
where the time goes in v2:
time: 163 us; the launch traced here: 162 us
  waiting for transfers between devices  47.3 us (29%)
  blocking collectives  43.3 us (27%)
  starting transfers between devices  41.6 us (26%)
  Pallas kernels  24.5 us (15%)
  between operations  1.86 us (1%)
  local copies, waits for them, and re-layouts  1.75 us (1%)
    ppermute x23, waiting for transfers between devices, send(): return lax.ppermute(a, 'col', perm)  41.6 us
    ppermute x23, starting transfers between devices, send(): return lax.ppermute(a, 'col', perm)  37.1 us
    all_to_all x1, blocking collectives, body(): lax.all_to_all(partial.reshape(ROWS * F, F), 'row', 0, 0, tiled=True)  22.5 us
    all_to_all x1, blocking collectives, body(): lax.all_to_all(outgoing.reshape(ROWS * SEND, BS), 'row', 0, 0, tiled=True)  20.8 us
    pallas_call x2, Pallas kernels, run(): call(functools.partial(kernel, first), out, specs, name, 48, scratch=scra...  10.8 us
    pallas_call x2, Pallas kernels, run(): call(functools.partial(backward_kernel, first), jax.ShapeDtypeStruct((gro...  10.7 us
    ppermute x4, waiting for transfers between devices, across(): return lax.ppermute(a, 'row', [(r, r ^ k) for r in range(ROWS)])  5.79 us
    ppermute x4, starting transfers between devices, across(): return lax.ppermute(a, 'row', [(r, r ^ k) for r in range(ROWS)])  4.49 us
  transfers between devices with their start and end apart: 27, of which 13 were waited for; matrix products, arithmetic and copies ran while one was open for 1% of the time, Pallas kernels for 10%

profile of v2, /device:TPU:4, one launch (start us, length us, event | category | flops | bytes accessed | tf_op | source)
XLA Modules:
  0.0 161.6 jit_solution(2425312514819021412)
XLA Ops:
  4.8 3.7 %collective-permute-done = bf16[256,256]{1,0:T(8,128)(2,1)S(1)} collective-permute-done((bf16[256,256]{1,0:T(8,128)(2,1)S(1)}, bf16[256,256]{1,0:T(8,128)(2,1)S(1)}, u32[]{:S(2)}, u32[]{:S(2)}) %collective-permute-start) | collective-permute-done | bytes 131104 | tf_op jit(solution)/shard_map/ppermute | solution.py:175
  10.5 4.0 %collective-permute-start.2 = (bf16[512,256]{1,0:T(8,128)(2,1)S(1)}, bf16[512,256]{1,0:T(8,128)(2,1)S(1)}, u32[]{:S(2)}, u32[]{:S(2)}) collective-permute-start(bf16[512,256]{1,0:T(8,128)(2,1)S(1)} %pad_maximum_fusion.4), channel_id=1, source_target_pairs={{0,14},{1,15},{2,0},{3,1},{4,2},{5,3},{6,4},{7,5},{8,6},{9,7},{10,... | collective-permute-start | bytes 786440 | tf_op jit(solution)/shard_map/ppermute | solution.py:175
  14.5 6.3 %collective-permute-done.1 = bf16[512,256]{1,0:T(8,128)(2,1)S(1)} collective-permute-done((bf16[512,256]{1,0:T(8,128)(2,1)S(1)}, bf16[512,256]{1,0:T(8,128)(2,1)S(1)}, u32[]{:S(2)}, u32[]{:S(2)}) %collective-permute-start.1) | collective-permute-done | bytes 262176 | tf_op jit(solution)/shard_map/ppermute | solution.py:175
  20.7 3.2 %collective-permute-start.4 = (bf16[512,256]{1,0:T(8,128)(2,1)S(1)}, bf16[512,256]{1,0:T(8,128)(2,1)S(1)}, u32[]{:S(2)}, u32[]{:S(2)}) collective-permute-start(bf16[512,256]{1,0:T(8,128)(2,1)S(1)} %collective-permute-done.2), channel_id=1, source_target_pairs={{0,14},{1,15},{2,0},{3,1},{4,2},{5,3},{6,4},{7,5},{8,6},{9,7},{10,... | collective-permute-start | bytes 786440 | tf_op jit(solution)/shard_map/ppermute | solution.py:175
  24.1 5.4 %collective-permute-done.3 = bf16[512,256]{1,0:T(8,128)(2,1)S(1)} collective-permute-done((bf16[512,256]{1,0:T(8,128)(2,1)S(1)}, bf16[512,256]{1,0:T(8,128)(2,1)S(1)}, u32[]{:S(2)}, u32[]{:S(2)}) %collective-permute-start.3) | collective-permute-done | bytes 262176 | tf_op jit(solution)/shard_map/ppermute | solution.py:175
  29.5 3.2 %collective-permute-start.6 = (bf16[512,256]{1,0:T(8,128)(2,1)S(1)}, bf16[512,256]{1,0:T(8,128)(2,1)S(1)}, u32[]{:S(2)}, u32[]{:S(2)}) collective-permute-start(bf16[512,256]{1,0:T(8,128)(2,1)S(1)} %collective-permute-done.4), channel_id=1, source_target_pairs={{0,14},{1,15},{2,0},{3,1},{4,2},{5,3},{6,4},{7,5},{8,6},{9,7},{10,... | collective-permute-start | bytes 786440 | tf_op jit(solution)/shard_map/ppermute | solution.py:175
  32.8 4.5 %collective-permute-done.5 = bf16[512,256]{1,0:T(8,128)(2,1)S(1)} collective-permute-done((bf16[512,256]{1,0:T(8,128)(2,1)S(1)}, bf16[512,256]{1,0:T(8,128)(2,1)S(1)}, u32[]{:S(2)}, u32[]{:S(2)}) %collective-permute-start.5) | collective-permute-done | bytes 262176 | tf_op jit(solution)/shard_map/ppermute | solution.py:175
  37.4 3.3 %collective-permute-start.8 = (bf16[256,256]{1,0:T(8,128)(2,1)S(1)}, bf16[256,256]{1,0:T(8,128)(2,1)S(1)}, u32[]{:S(2)}, u32[]{:S(2)}) collective-permute-start(bf16[256,256]{1,0:T(8,128)(2,1)S(1)} %slice.178), channel_id=1, source_target_pairs={{0,14},{1,15},{2,0},{3,1},{4,2},{5,3},{6,4},{7,5},{8,6},{9,7},{10,... | collective-permute-start | bytes 393224 | tf_op jit(solution)/shard_map/ppermute | solution.py:175
  40.8 2.8 %collective-permute-done.7 = bf16[256,256]{1,0:T(8,128)(2,1)S(1)} collective-permute-done((bf16[256,256]{1,0:T(8,128)(2,1)S(1)}, bf16[256,256]{1,0:T(8,128)(2,1)S(1)}, u32[]{:S(2)}, u32[]{:S(2)}) %collective-permute-start.7) | collective-permute-done | bytes 131104 | tf_op jit(solution)/shard_map/ppermute | solution.py:175
  44.7 4.9 %forward_1.1.begun = f32[17,128,256]{2,1,0:T(8,128)S(1)} custom-call(s32[32]{0:T(128)S(1)} %fusion.11.ids, s32[256]{0:T(256)S(1)} %reshape_squeeze.6.src, s32[256]{0:T(256)S(1)} %get-tuple-element.37.dst, bf16[16,256,256]{2,1,0:T(8,128)(2,1)S(1)} %bitcast.50, bf16[32,8,128,128]{3,2,1,0:T(8,128)(2,1)} %bitcast.53), custom_call_target="tpu_custom_call" | custom-call | flops 1073741824 | bytes 16777216 | tf_op jit(solution)/shard_map/forward_1/pallas_call | solution.py:225
  49.6 5.9 %forward_2.1 = bf16[16,128,256]{2,1,0:T(8,128)(2,1)S(1)} custom-call(s32[32]{0:T(128)S(1)} %fusion.11.ids, s32[256]{0:T(256)S(1)} %reshape_squeeze.6.src, s32[256]{0:T(256)S(1)} %get-tuple-element.37.dst, bf16[16,256,256]{2,1,0:T(8,128)(2,1)} %bitcast.2.x, bf16[32,8,128,128]{3,2,1,0:T(8,128)(2,1)} %bitcast.54, f32[17,128,256]{2,1,0:T(8,128)S(1)} %forward_1.1.begun), custom_call_target="tpu_custom_call" | custom-call | flops 1073741824 | bytes 16777216 | tf_op jit(solution)/shard_map/forward_2/pallas_call | solution.py:225
  55.5 22.5 %all_to_all.15.recv = bf16[8,256,256]{2,1,0:T(8,128)(2,1)S(1)} all-to-all(bf16[8,256,256]{2,1,0:T(8,128)(2,1)S(1)} %bitcast.49), channel_id=1, replica_groups=mesh['row'=8,'col'=32] {'row'}, dimensions={0} | all-to-all | bytes 2097152 | tf_op jit(solution)/shard_map/all_to_all | solution.py:309
  79.0 20.8 %all_to_all.16.recv = bf16[8,576,128]{2,1,0:T(8,128)(2,1)S(1)} all-to-all(bf16[8,576,128]{2,1,0:T(8,128)(2,1)S(1)} %get-tuple-element.10), channel_id=1, replica_groups=mesh['row'=8,'col'=32] {'row'}, dimensions={0} | all-to-all | bytes 2359296 | tf_op jit(solution)/shard_map/all_to_all | solution.py:314
  100.7 5.4 %backward_1.1 = bf16[16,512,128]{2,1,0:T(8,128)(2,1)S(1)} custom-call(s32[32]{0:T(128)S(1)} %fusion.11.ids, s32[256]{0:T(256)S(1)} %get-tuple-element.36.code, s32[256]{0:T(256)S(1)} %reshape_squeeze.7.dst, bf16[8,576,128]{2,1,0:T(8,128)(2,1)S(1)} %all_to_all.16.recv, bf16[32,8,128,128]{3,2,1,0:T(8,128)(2,1)} %bitcast.55), custom_call_target="tpu_custom_call" | custom-call | flops 1073741824 | bytes 16777216 | tf_op jit(solution)/shard_map/backward_1/pallas_call | solution.py:246
  106.6 5.4 %backward_2.1 = bf16[16,512,128]{2,1,0:T(8,128)(2,1)S(1)} custom-call(s32[32]{0:T(128)S(1)} %fusion.11.ids, s32[256]{0:T(256)S(1)} %get-tuple-element.36.code, s32[256]{0:T(256)S(1)} %reshape_squeeze.7.dst, bf16[8,576,128]{2,1,0:T(8,128)(2,1)S(1)} %all_to_all.16.recv, bf16[32,8,128,128]{3,2,1,0:T(8,128)(2,1)} %bitcast.56), custom_call_target="tpu_custom_call" | custom-call | flops 1073741824 | bytes 16777216 | tf_op jit(solution)/shard_map/backward_2/pallas_call | solution.py:246
  112.6 3.4 %collective-permute-start.17 = (bf16[576,128]{1,0:T(8,128)(2,1)S(1)}, bf16[576,128]{1,0:T(8,128)(2,1)S(1)}, u32[]{:S(2)}, u32[]{:S(2)}) collective-permute-start(bf16[576,128]{1,0:T(8,128)(2,1)S(1)} %get-tuple-element.35), channel_id=1, source_target_pairs={{0,14},{1,15},{2,0},{3,1},{4,2},{5,3},{6,4},{7,5},{8,6},{9,7},{10,... | collective-permute-start | bytes 442376 | tf_op jit(solution)/shard_map/ppermute | solution.py:175
  116.0 3.8 %collective-permute-done.13 = bf16[576,128]{1,0:T(8,128)(2,1)S(1)} collective-permute-done((bf16[576,128]{1,0:T(8,128)(2,1)S(1)}, bf16[576,128]{1,0:T(8,128)(2,1)S(1)}, u32[]{:S(2)}, u32[]{:S(2)}) %collective-permute-start.13) | collective-permute-done | bytes 147488 | tf_op jit(solution)/shard_map/ppermute | solution.py:175
  120.2 3.3 %collective-permute-start.18 = (bf16[1088,128]{1,0:T(8,128)(2,1)S(1)}, bf16[1088,128]{1,0:T(8,128)(2,1)S(1)}, u32[]{:S(2)}, u32[]{:S(2)}) collective-permute-start(bf16[1088,128]{1,0:T(8,128)(2,1)S(1)} %pad_maximum_fusion.2), channel_id=1, source_target_pairs={{0,14},{1,15},{2,0},{3,1},{4,2},{5,3},{6,4},{7,5},{8,6},{9,7},{10,... | collective-permute-start | bytes 835592 | tf_op jit(solution)/shard_map/ppermute | solution.py:175
  123.5 6.2 %collective-permute-done.14 = bf16[1088,128]{1,0:T(8,128)(2,1)S(1)} collective-permute-done((bf16[1088,128]{1,0:T(8,128)(2,1)S(1)}, bf16[1088,128]{1,0:T(8,128)(2,1)S(1)}, u32[]{:S(2)}, u32[]{:S(2)}) %collective-permute-start.14) | collective-permute-done | bytes 278560 | tf_op jit(solution)/shard_map/ppermute | solution.py:175
  129.9 3.3 %collective-permute-start.19 = (bf16[1088,128]{1,0:T(8,128)(2,1)S(1)}, bf16[1088,128]{1,0:T(8,128)(2,1)S(1)}, u32[]{:S(2)}, u32[]{:S(2)}) collective-permute-start(bf16[1088,128]{1,0:T(8,128)(2,1)S(1)} %pad_maximum_fusion.3), channel_id=1, source_target_pairs={{0,14},{1,15},{2,0},{3,1},{4,2},{5,3},{6,4},{7,5},{8,6},{9,7},{10,... | collective-permute-start | bytes 835592 | tf_op jit(solution)/shard_map/ppermute | solution.py:175
  133.2 3.2 %collective-permute-start.22 = (bf16[64,128]{1,0:T(8,128)(2,1)S(1)}, bf16[64,128]{1,0:T(8,128)(2,1)S(1)}, u32[]{:S(2)}, u32[]{:S(2)}) collective-permute-start(bf16[64,128]{1,0:T(8,128)(2,1)S(1)} %add_convert_fusion.2.refs_0_), channel_id=1, source_target_pairs={{0,8},{1,9},{2,10},{3,11},{4,12},{5,13},{6,14},{7,15},{8,0},{9,1},... | collective-permute-start | bytes 49160 | tf_op jit(solution)/shard_map/ppermute | solution.py:175
  136.4 2.7 %collective-permute-done.15 = bf16[1088,128]{1,0:T(8,128)(2,1)S(1)} collective-permute-done((bf16[1088,128]{1,0:T(8,128)(2,1)S(1)}, bf16[1088,128]{1,0:T(8,128)(2,1)S(1)}, u32[]{:S(2)}, u32[]{:S(2)}) %collective-permute-start.15) | collective-permute-done | bytes 278560 | tf_op jit(solution)/shard_map/ppermute | solution.py:175
  150.4 3.2 %collective-permute-done.25 = bf16[128,128]{1,0:T(8,128)(2,1)S(1)} collective-permute-done((bf16[128,128]{1,0:T(8,128)(2,1)S(1)}, bf16[128,128]{1,0:T(8,128)(2,1)S(1)}, u32[]{:S(2)}, u32[]{:S(2)}) %collective-permute-start.25) | collective-permute-done | bytes 32800 | tf_op jit(solution)/shard_map/ppermute | solution.py:179
  157.3 2.9 %collective-permute-done.21.b = bf16[512,128]{1,0:T(8,128)(2,1)S(1)} collective-permute-done((bf16[512,128]{1,0:T(8,128)(2,1)S(1)}, bf16[512,128]{1,0:T(8,128)(2,1)S(1)}, u32[]{:S(2)}, u32[]{:S(2)}) %collective-permute-start.21) | collective-permute-done | bytes 131104 | tf_op jit(solution)/shard_map/ppermute | solution.py:175
  (110 shorter events, 26.6 us)
Async XLA Ops:
  2.2 6.2 %collective-permute-start = (bf16[256,256]{1,0:T(8,128)(2,1)S(1)}, bf16[256,256]{1,0:T(8,128)(2,1)S(1)}, u32[]{:S(2)}, u32[]{:S(2)}) collective-permute-start(bf16[256,256]{1,0:T(8,128)(2,1)S(1)} %maximum_select_fusion), channel_id=1, source_target_pairs={{0,16},{1,17},{2,18},{3,19},{4,20},{5,21},{6,22},{7,23},{8,24},{9,... | collective-permute-start | bytes 393224 | tf_op jit(solution)/shard_map/ppermute | solution.py:175
  8.5 12.3 %collective-permute-start.1 = (bf16[512,256]{1,0:T(8,128)(2,1)S(1)}, bf16[512,256]{1,0:T(8,128)(2,1)S(1)}, u32[]{:S(2)}, u32[]{:S(2)}) collective-permute-start(bf16[512,256]{1,0:T(8,128)(2,1)S(1)} %pad_maximum_fusion.4), channel_id=1, source_target_pairs={{0,2},{1,3},{2,4},{3,5},{4,6},{5,7},{6,8},{7,9},{8,10},{9,11},{10,... | collective-permute-start | bytes 786440 | tf_op jit(solution)/shard_map/ppermute | solution.py:175
  10.5 10.3 %collective-permute-start.2 = (bf16[512,256]{1,0:T(8,128)(2,1)S(1)}, bf16[512,256]{1,0:T(8,128)(2,1)S(1)}, u32[]{:S(2)}, u32[]{:S(2)}) collective-permute-start(bf16[512,256]{1,0:T(8,128)(2,1)S(1)} %pad_maximum_fusion.4), channel_id=1, source_target_pairs={{0,14},{1,15},{2,0},{3,1},{4,2},{5,3},{6,4},{7,5},{8,6},{9,7},{10,... | collective-permute-start | bytes 786440 | tf_op jit(solution)/shard_map/ppermute | solution.py:175
  20.7 8.7 %collective-permute-start.3 = (bf16[512,256]{1,0:T(8,128)(2,1)S(1)}, bf16[512,256]{1,0:T(8,128)(2,1)S(1)}, u32[]{:S(2)}, u32[]{:S(2)}) collective-permute-start(bf16[512,256]{1,0:T(8,128)(2,1)S(1)} %collective-permute-done.1), channel_id=1, source_target_pairs={{0,2},{1,3},{2,4},{3,5},{4,6},{5,7},{6,8},{7,9},{8,10},{9,11},{10,... | collective-permute-start | bytes 786440 | tf_op jit(solution)/shard_map/ppermute | solution.py:175
  20.7 8.7 %collective-permute-start.4 = (bf16[512,256]{1,0:T(8,128)(2,1)S(1)}, bf16[512,256]{1,0:T(8,128)(2,1)S(1)}, u32[]{:S(2)}, u32[]{:S(2)}) collective-permute-start(bf16[512,256]{1,0:T(8,128)(2,1)S(1)} %collective-permute-done.2), channel_id=1, source_target_pairs={{0,14},{1,15},{2,0},{3,1},{4,2},{5,3},{6,4},{7,5},{8,6},{9,7},{10,... | collective-permute-start | bytes 786440 | tf_op jit(solution)/shard_map/ppermute | solution.py:175
  29.5 7.8 %collective-permute-start.5 = (bf16[512,256]{1,0:T(8,128)(2,1)S(1)}, bf16[512,256]{1,0:T(8,128)(2,1)S(1)}, u32[]{:S(2)}, u32[]{:S(2)}) collective-permute-start(bf16[512,256]{1,0:T(8,128)(2,1)S(1)} %collective-permute-done.3), channel_id=1, source_target_pairs={{0,2},{1,3},{2,4},{3,5},{4,6},{5,7},{6,8},{7,9},{8,10},{9,11},{10,... | collective-permute-start | bytes 786440 | tf_op jit(solution)/shard_map/ppermute | solution.py:175
  29.5 7.9 %collective-permute-start.6 = (bf16[512,256]{1,0:T(8,128)(2,1)S(1)}, bf16[512,256]{1,0:T(8,128)(2,1)S(1)}, u32[]{:S(2)}, u32[]{:S(2)}) collective-permute-start(bf16[512,256]{1,0:T(8,128)(2,1)S(1)} %collective-permute-done.4), channel_id=1, source_target_pairs={{0,14},{1,15},{2,0},{3,1},{4,2},{5,3},{6,4},{7,5},{8,6},{9,7},{10,... | collective-permute-start | bytes 786440 | tf_op jit(solution)/shard_map/ppermute | solution.py:175
  37.3 6.3 %collective-permute-start.7 = (bf16[256,256]{1,0:T(8,128)(2,1)S(1)}, bf16[256,256]{1,0:T(8,128)(2,1)S(1)}, u32[]{:S(2)}, u32[]{:S(2)}) collective-permute-start(bf16[256,256]{1,0:T(8,128)(2,1)S(1)} %slice.177), channel_id=1, source_target_pairs={{0,2},{1,3},{2,4},{3,5},{4,6},{5,7},{6,8},{7,9},{8,10},{9,11},{10,... | collective-permute-start | bytes 393224 | tf_op jit(solution)/shard_map/ppermute | solution.py:175
  37.4 6.2 %collective-permute-start.8 = (bf16[256,256]{1,0:T(8,128)(2,1)S(1)}, bf16[256,256]{1,0:T(8,128)(2,1)S(1)}, u32[]{:S(2)}, u32[]{:S(2)}) collective-permute-start(bf16[256,256]{1,0:T(8,128)(2,1)S(1)} %slice.178), channel_id=1, source_target_pairs={{0,14},{1,15},{2,0},{3,1},{4,2},{5,3},{6,4},{7,5},{8,6},{9,7},{10,... | collective-permute-start | bytes 393224 | tf_op jit(solution)/shard_map/ppermute | solution.py:175
  43.6 6.0 %collective-permute-start.9 = (bf16[4096,256]{1,0:T(8,128)(2,1)S(1)}, bf16[4096,256]{1,0:T(8,128)(2,1)}, u32[]{:S(2)}, u32[]{:S(2)}) collective-permute-start(bf16[4096,256]{1,0:T(8,128)(2,1)S(1)} %constant_dynamic-update-slice_fusion), channel_id=1, source_target_pairs={{0,1},{1,0},{2,3},{3,2},{4,5},{5,4},{6,7},{7,6},{8,9},{9,8},{10,11... | collective-permute-start | bytes 6291464 | tf_op jit(solution)/shard_map/ppermute | solution.py:175
  99.9 6.2 %collective-permute-start.10 = (f32[64,128]{1,0:T(8,128)S(1)}, f32[64,128]{1,0:T(8,128)S(1)}, u32[]{:S(2)}, u32[]{:S(2)}) collective-permute-start(f32[64,128]{1,0:T(8,128)S(1)} %convert_reduce_fusion), channel_id=1, source_target_pairs={{0,16},{1,17},{2,18},{3,19},{4,20},{5,21},{6,22},{7,23},{8,24},{9,... | collective-permute-start | bytes 98312 | tf_op jit(solution)/shard_map/ppermute | solution.py:175
  106.0 6.0 %collective-permute-start.11 = (bf16[16,512,128]{2,1,0:T(8,128)(2,1)S(1)}, bf16[16,512,128]{2,1,0:T(8,128)(2,1)S(1)}, u32[]{:S(2)}, u32[]{:S(2)}) collective-permute-start(bf16[16,512,128]{2,1,0:T(8,128)(2,1)S(1)} %backward_1.1), channel_id=1, source_target_pairs={{0,1},{1,0},{2,3},{3,2},{4,5},{5,4},{6,7},{7,6},{8,9},{9,8},{10,11... | collective-permute-start | bytes 6291464 | tf_op jit(solution)/shard_map/ppermute | solution.py:175
  106.1 5.9 %collective-permute-start.12 = (f32[64,128]{1,0:T(8,128)S(1)}, f32[64,128]{1,0:T(8,128)S(1)}, u32[]{:S(2)}, u32[]{:S(2)}) collective-permute-start(f32[64,128]{1,0:T(8,128)S(1)} %add.105), channel_id=1, source_target_pairs={{0,1},{1,0},{2,3},{3,2},{4,5},{5,4},{6,7},{7,6},{8,9},{9,8},{10,11... | collective-permute-start | bytes 98312 | tf_op jit(solution)/shard_map/ppermute | solution.py:175
  112.1 7.7 %collective-permute-start.13 = (bf16[576,128]{1,0:T(8,128)(2,1)S(1)}, bf16[576,128]{1,0:T(8,128)(2,1)S(1)}, u32[]{:S(2)}, u32[]{:S(2)}) collective-permute-start(bf16[576,128]{1,0:T(8,128)(2,1)S(1)} %get-tuple-element.34), channel_id=1, source_target_pairs={{0,2},{1,3},{2,4},{3,5},{4,6},{5,7},{6,8},{7,9},{8,10},{9,11},{10,... | collective-permute-start | bytes 442376 | tf_op jit(solution)/shard_map/ppermute | solution.py:175
  112.6 7.4 %collective-permute-start.17 = (bf16[576,128]{1,0:T(8,128)(2,1)S(1)}, bf16[576,128]{1,0:T(8,128)(2,1)S(1)}, u32[]{:S(2)}, u32[]{:S(2)}) collective-permute-start(bf16[576,128]{1,0:T(8,128)(2,1)S(1)} %get-tuple-element.35), channel_id=1, source_target_pairs={{0,14},{1,15},{2,0},{3,1},{4,2},{5,3},{6,4},{7,5},{8,6},{9,7},{10,... | collective-permute-start | bytes 442376 | tf_op jit(solution)/shard_map/ppermute | solution.py:175
  119.9 9.7 %collective-permute-start.14 = (bf16[1088,128]{1,0:T(8,128)(2,1)S(1)}, bf16[1088,128]{1,0:T(8,128)(2,1)S(1)}, u32[]{:S(2)}, u32[]{:S(2)}) collective-permute-start(bf16[1088,128]{1,0:T(8,128)(2,1)S(1)} %pad_maximum_fusion), channel_id=1, source_target_pairs={{0,2},{1,3},{2,4},{3,5},{4,6},{5,7},{6,8},{7,9},{8,10},{9,11},{10,... | collective-permute-start | bytes 835592 | tf_op jit(solution)/shard_map/ppermute | solution.py:175
  120.2 9.7 %collective-permute-start.18 = (bf16[1088,128]{1,0:T(8,128)(2,1)S(1)}, bf16[1088,128]{1,0:T(8,128)(2,1)S(1)}, u32[]{:S(2)}, u32[]{:S(2)}) collective-permute-start(bf16[1088,128]{1,0:T(8,128)(2,1)S(1)} %pad_maximum_fusion.2), channel_id=1, source_target_pairs={{0,14},{1,15},{2,0},{3,1},{4,2},{5,3},{6,4},{7,5},{8,6},{9,7},{10,... | collective-permute-start | bytes 835592 | tf_op jit(solution)/shard_map/ppermute | solution.py:175
  129.7 9.3 %collective-permute-start.15 = (bf16[1088,128]{1,0:T(8,128)(2,1)S(1)}, bf16[1088,128]{1,0:T(8,128)(2,1)S(1)}, u32[]{:S(2)}, u32[]{:S(2)}) collective-permute-start(bf16[1088,128]{1,0:T(8,128)(2,1)S(1)} %pad_maximum_fusion.1), channel_id=1, source_target_pairs={{0,2},{1,3},{2,4},{3,5},{4,6},{5,7},{6,8},{7,9},{8,10},{9,11},{10,... | collective-permute-start | bytes 835592 | tf_op jit(solution)/shard_map/ppermute | solution.py:175
  129.9 9.1 %collective-permute-start.19 = (bf16[1088,128]{1,0:T(8,128)(2,1)S(1)}, bf16[1088,128]{1,0:T(8,128)(2,1)S(1)}, u32[]{:S(2)}, u32[]{:S(2)}) collective-permute-start(bf16[1088,128]{1,0:T(8,128)(2,1)S(1)} %pad_maximum_fusion.3), channel_id=1, source_target_pairs={{0,14},{1,15},{2,0},{3,1},{4,2},{5,3},{6,4},{7,5},{8,6},{9,7},{10,... | collective-permute-start | bytes 835592 | tf_op jit(solution)/shard_map/ppermute | solution.py:175
  133.2 7.6 %collective-permute-start.22 = (bf16[64,128]{1,0:T(8,128)(2,1)S(1)}, bf16[64,128]{1,0:T(8,128)(2,1)S(1)}, u32[]{:S(2)}, u32[]{:S(2)}) collective-permute-start(bf16[64,128]{1,0:T(8,128)(2,1)S(1)} %add_convert_fusion.2.refs_0_), channel_id=1, source_target_pairs={{0,8},{1,9},{2,10},{3,11},{4,12},{5,13},{6,14},{7,15},{8,0},{9,1},... | collective-permute-start | bytes 49160 | tf_op jit(solution)/shard_map/ppermute | solution.py:175
  142.0 11.5 %collective-permute-start.20 = (bf16[1024,128]{1,0:T(8,128)(2,1)S(1)}, bf16[1024,128]{1,0:T(8,128)(2,1)S(1)}, u32[]{:S(2)}, u32[]{:S(2)}) collective-permute-start(bf16[1024,128]{1,0:T(8,128)(2,1)S(1)} %fusion.2), channel_id=1, source_target_pairs={{0,14},{1,15},{2,0},{3,1},{4,2},{5,3},{6,4},{7,5},{8,6},{9,7},{10,... | collective-permute-start | bytes 786440 | tf_op jit(solution)/shard_map/ppermute | solution.py:175
  147.4 7.7 %collective-permute-start.16 = (bf16[1024,128]{1,0:T(8,128)(2,1)S(1)}, bf16[1024,128]{1,0:T(8,128)(2,1)S(1)}, u32[]{:S(2)}, u32[]{:S(2)}) collective-permute-start(bf16[1024,128]{1,0:T(8,128)(2,1)S(1)} %fusion.5), channel_id=1, source_target_pairs={{0,2},{1,3},{2,4},{3,5},{4,6},{5,7},{6,8},{7,9},{8,10},{9,11},{10,... | collective-permute-start | bytes 786440 | tf_op jit(solution)/shard_map/ppermute | solution.py:175
  148.0 5.5 %collective-permute-start.25 = (bf16[128,128]{1,0:T(8,128)(2,1)S(1)}, bf16[128,128]{1,0:T(8,128)(2,1)S(1)}, u32[]{:S(2)}, u32[]{:S(2)}) collective-permute-start(bf16[128,128]{1,0:T(8,128)(2,1)S(1)} %pad_maximum_fusion.7), channel_id=1, source_target_pairs={{0,128},{32,160},{64,192},{96,224},{128,0},{160,32},{192,64},{224,... | collective-permute-start | bytes 98312 | tf_op jit(solution)/shard_map/ppermute | solution.py:179
  149.5 7.2 %collective-permute-start.26 = (bf16[128,128]{1,0:T(8,128)(2,1)S(1)}, bf16[128,128]{1,0:T(8,128)(2,1)S(1)}, u32[]{:S(2)}, u32[]{:S(2)}) collective-permute-start(bf16[128,128]{1,0:T(8,128)(2,1)S(1)} %pad_maximum_fusion.7), channel_id=1, source_target_pairs={{0,192},{32,224},{64,128},{96,160},{128,64},{160,96},{192,0},{224,... | collective-permute-start | bytes 98312 | tf_op jit(solution)/shard_map/ppermute | solution.py:179
  (10 other events, 158.6 us)
